TPU v7x, 32 devices: a whole 2x2x4 slice. The times are simulated.
32 devices in a mesh: row: 4 (over z), col: 8 (over y, x, core).
Axes of the slice: x: 2, y: 2, z: 4, core: 2. Of those that a mesh axis runs over, the one named last changes fastest.
Arguments:
- student_in: bfloat16 [64, 8192], P('col', 'row'), may hold values from -260 to 260
- teacher_hidden: bfloat16 [64, 16384], P(None, 'col'), may hold values from -1600 to 1600
- proj: bfloat16 [16384, 8192], P('col', 'row'), may hold values from -0.046875 to 0.046875
- w_gate: bfloat16 [8192, 28672], P('row', 'col'), may hold values from -0.0625 to 0.0625
- w_up: bfloat16 [8192, 28672], P('row', 'col'), may hold values from -0.0625 to 0.0625
- w_down: bfloat16 [28672, 8192], P('col', 'row'), may hold values from -0.03125 to 0.03125
Outputs:
- grad_gate: bfloat16 [8192, 28672], P('row', 'col')
- grad_up: bfloat16 [8192, 28672], P('row', 'col')
- grad_down: bfloat16 [28672, 8192], P('col', 'row')
- distill_loss: float32 [], replicated
All inputs are finite; a program needn't handle non-finite values.
Results may differ from a plain program's by a relative error of at most 0.0099.
Values may be sent and summed in bfloat16 or wider, within the bound.
No kernel may reach another device: no remote copies, remote signals or barrier semaphores. Data moves between devices by JAX's collectives and lax.ppermute only.
A program may use at most 192 MiB of HBM per device.

v0:
```python
import jax
import jax.numpy as jnp
from jax import lax
from jax.sharding import PartitionSpec as P


def merged_2(array, axis, combine):
    everything = jax.tree.map(lambda part: lax.all_gather(part, axis), array)
    leading = jax.tree.map(lambda part: part[0], everything)

    def turn(k, so_far):
        return combine(so_far, jax.tree.map(lambda part: part[k], everything))

    return lax.fori_loop(1, lax.axis_size(axis), turn, leading)


def activate(gate_full, width_ff):
    gate_val = gate_full[:, :width_ff]
    up_val = gate_full[:, width_ff:]
    logistic = jax.nn.sigmoid(gate_val)
    silu_gate = gate_val * logistic
    hidden = (silu_gate * up_val).astype(jnp.bfloat16)
    return (gate_val, up_val, logistic, silu_gate, hidden)


def backward_pair(hidden_grad, gate_val, up_val, logistic, silu_gate):
    slope = logistic * (1.0 + gate_val * (1.0 - logistic))
    gate_grad = (hidden_grad * up_val * slope).astype(jnp.bfloat16)
    up_grad = (hidden_grad * silu_gate).astype(jnp.bfloat16)
    return jnp.concatenate([gate_grad, up_grad], axis=1)


def join_parts(first, second):
    stud_max = jnp.maximum(first[0], second[0])
    stud_norm = first[1] * jnp.exp(first[0] - stud_max) + second[1] * jnp.exp(second[0] - stud_max)
    teach_max = jnp.maximum(first[2], second[2])
    scale_one = jnp.exp(first[2] - teach_max)
    scale_two = jnp.exp(second[2] - teach_max)
    teach_norm = first[3] * scale_one + second[3] * scale_two
    cross_sum = first[4] * scale_one + second[4] * scale_two
    return (stud_max, stud_norm, teach_max, teach_norm, cross_sum)


def local(student_in, teacher_hidden, proj, w_gate, w_up, w_down):
    width_ff = w_gate.shape[1]
    tok_rows = lax.all_gather(student_in, "col", axis=0, tiled=True)
    gate_up = jnp.concatenate([w_gate, w_up], axis=1)
    gate_part = jnp.dot(tok_rows, gate_up, preferred_element_type=jnp.float32)
    gate_full = lax.psum(gate_part, "row")
    gate_val, up_val, logistic, silu_gate, hidden = activate(gate_full, width_ff)
    teach_part = jnp.dot(teacher_hidden, proj, preferred_element_type=jnp.float32)
    stud_part = jnp.dot(hidden, w_down, preferred_element_type=jnp.float32)
    stud_sum, teacher = lax.psum((stud_part, teach_part), "col")
    student = tok_rows.astype(jnp.float32) + stud_sum
    local_smax = jnp.max(student, axis=1)
    local_snorm = jnp.sum(jnp.exp(student - local_smax[:, None]), axis=1)
    local_tmax = jnp.max(teacher, axis=1)
    teach_exp = jnp.exp(teacher - local_tmax[:, None])
    local_tnorm = jnp.sum(teach_exp, axis=1)
    local_cross = jnp.sum(teach_exp * student, axis=1)
    merged = merged_2(
        (local_smax, local_snorm, local_tmax, local_tnorm, local_cross), "row", join_parts
    )
    stud_max, stud_norm, teach_max, teach_norm, cross_sum = merged
    token_loss = stud_max + jnp.log(stud_norm) - cross_sum / teach_norm
    stud_probs = jnp.exp(student - stud_max[:, None]) / stud_norm[:, None]
    teach_probs = jnp.exp(teacher - teach_max[:, None]) / teach_norm[:, None]
    stud_grad = (stud_probs - teach_probs).astype(jnp.bfloat16)
    distill_loss = jnp.mean(token_loss)
    grad_down = lax.dot_general(
        hidden, stud_grad, (((0,), (0,)), ((), ())), preferred_element_type=jnp.float32
    ).astype(jnp.bfloat16)
    hidden_part = lax.dot_general(
        stud_grad, w_down, (((1,), (1,)), ((), ())), preferred_element_type=jnp.float32
    )
    hidden_grad = lax.psum(hidden_part, "row")
    grad_pair = backward_pair(hidden_grad, gate_val, up_val, logistic, silu_gate)
    both_grads = lax.dot_general(
        tok_rows, grad_pair, (((0,), (0,)), ((), ())), preferred_element_type=jnp.float32
    ).astype(jnp.bfloat16)
    return (both_grads[:, :width_ff], both_grads[:, width_ff:], grad_down, distill_loss)


def solution(mesh):
    return jax.shard_map(
        local,
        mesh=mesh,
        in_specs=(
            P("col", "row"),
            P(None, "col"),
            P("col", "row"),
            P("row", "col"),
            P("row", "col"),
            P("col", "row"),
        ),
        out_specs=(P("row", "col"), P("row", "col"), P("col", "row"), P()),
        check_vma=False,
    )
```

profile of v0, /device:TPU:0, one launch (start us, length us, event | category | flops | bytes accessed | tf_op | source)
XLA Modules:
  0.0 331.8 jit_solution(18020471315865150923)
XLA Ops:
  7.2 11.1 %all_gather.33 = bf16[64,2048]{1,0:T(8,128)(2,1)S(1)} all-gather(bf16[8,2048]{1,0:T(8,128)(2,1)} %param.8), channel_id=1, replica_groups=mesh['row'=4,'col'=8] {'col'}, dimensions={0}, use_global_device_ids=true | all-gather | bytes 294912 | tf_op jit(solution)/shard_map/all_gather | solution.py:46
  18.3 12.6 %fusion.17 = f32[64,7168]{1,0:T(8,128)} fusion(bf16[64,2048]{1,0:T(8,128)(2,1)S(1)} %all_gather.33, bf16[2048,3584]{1,0:T(8,128)(2,1)} %param.12, bf16[2048,3584]{1,0:T(8,128)(2,1)} %param.11), kind=kOutput, calls=%fused_computation.26 | convolution fusion | flops 1937768448 | bytes 31457280 | tf_op jit(solution)/shard_map/dot_general | solution.py:48
  31.0 5.7 %fusion.33 = f32[64,2048]{1,0:T(8,128)} fusion(bf16[64,2048]{1,0:T(8,128)(2,1)S(1)} %copy-done, bf16[2048,2048]{1,0:T(8,128)(2,1)} %param.10), kind=kOutput, calls=%fused_computation.48 | convolution fusion | flops 536870912 | bytes 9175040 | tf_op jit(solution)/shard_map/dot_general | solution.py:51
  36.8 72.3 %all-reduce.11.cloned.1.call-done = f32[64,7168]{1,0:T(8,128)} async-done(((f32[64,7168]{1,0:T(8,128)}), f32[64,7168]{1,0:T(8,128)}) %all-reduce.11.cloned.1.call-update) | async-done | bytes 1835024 | tf_op jit(solution)/shard_map/psum | solution.py:49
  109.1 1.7 multiply_convert_fusion.2
  110.8 0.8 copy-done.5
  111.6 8.7 %fusion.32 = f32[64,2048]{1,0:T(8,128)} fusion(bf16[64,3584]{1,0:T(8,128)(2,1)S(1)} %multiply_convert_fusion.2, bf16[3584,2048]{1,0:T(8,128)(2,1)} %param.13), kind=kOutput, calls=%fused_computation.47 | convolution fusion | flops 939524096 | bytes 15663104 | tf_op jit(solution)/shard_map/dot_general | solution.py:52
  120.4 0.6 dynamic-slice
  121.6 54.7 %all-reduce.15.cloned.1.call-done = (f32[64,2048]{1,0:T(8,128)}, f32[64,2048]{1,0:T(8,128)}) async-done(((f32[64,2048]{1,0:T(8,128)}, f32[64,2048]{1,0:T(8,128)}), (f32[64,2048]{1,0:T(8,128)}, f32[64,2048]{1,0:T(8,128)})) %all-reduce.15.cloned.1.call-update) | async-done | bytes 1048592 | tf_op jit(solution)/shard_map/psum | solution.py:53
  176.2 1.3 fusion.25
  177.5 1.2 reduce_max.19
  178.7 1.6 multiply_reduce_fusion
  180.4 0.2 dynamic-update-slice
  181.4 11.8 %all-reduce.6 = (f32[256]{0:T(256)S(1)}, f32[256]{0:T(256)S(1)}, f32[256]{0:T(256)S(1)}, f32[256]{0:T(256)S(1)}, f32[256]{0:T(256)S(1)}) all-reduce(f32[256]{0:T(256)S(1)} %dynamic-update-slice, f32[256]{0:T(256)S(1)} %dynamic-update-slice.1, f32[256]{0:T(256)S(1)} %dynamic-update-slice.2, ...), channel_id=2, replica_groups=mesh['row'=4,'col'=8] {'row'}, use_global_device_ids=true, to_apply=%add | all-reduce | flops 1280 | bytes 10240
  193.7 0.2 while.23
  193.9 11.1 %fusion.28 = f32[64,3584]{1,0:T(8,128)} fusion(bf16[3584,2048]{1,0:T(8,128)(2,1)} %param.13, f32[64,2048]{1,0:T(8,128)} %get-tuple-element.306, f32[64]{0:T(128)S(1)} %get-tuple-element.275, f32[64]{0:T(128)S(1)} %get-tuple-element.274, f32[64]{0:T(128)S(1)} %get-tuple-element.273, f32[64]{0:T(128)S(1)} %get-tuple-element.272, ...), kind=kOutput, calls=%fused_computation.45 | convolution fusion | flops 940572672 | bytes 16909312 | tf_op jit(solution)/shard_map/dot_general | solution.py:73
  205.0 0.6 subtract_reduce_fusion
  206.3 8.8 %convolution_convert_fusion = bf16[3584,2048]{1,0:T(8,128)(2,1)} fusion(bf16[64,3584]{1,0:T(8,128)(2,1)} %copy-done.5, f32[64,2048]{1,0:T(8,128)S(1)} %copy-done.2, f32[64]{0:T(128)S(1)} %get-tuple-element.275, f32[64]{0:T(128)S(1)} %get-tuple-element.274, f32[64]{0:T(128)S(1)} %get-tuple-element.273, f32[64]{0:T(128)S(1)} %get-tuple-element.272, ...), kind=kOutput, calls=%fused_computation.25 | convolution fusion | flops 947912704 | bytes 16450560 | tf_op jit(solution)/shard_map/dot_general | solution.py:70
  215.0 34.3 %all-reduce.13.cloned.1.call-done = f32[64,3584]{1,0:T(8,128)} async-done(((f32[64,3584]{1,0:T(8,128)}), f32[64,3584]{1,0:T(8,128)}) %all-reduce.13.cloned.1.call-update) | async-done | bytes 917520 | tf_op jit(solution)/shard_map/psum | solution.py:76
  249.4 1.6 multiply_convert_fusion.1
  251.0 13.6 %convert_bitcast_fusion = bf16[2048,7168]{0,1:T(8,128)(2,1)} fusion(bf16[64,2048]{1,0:T(8,128)(2,1)S(1)} %all_gather.33, bf16[64,3584]{1,0:T(8,128)(2,1)S(1)} %get-tuple-element.321, bf16[64,3584]{1,0:T(8,128)(2,1)S(1)} %get-tuple-element.320), kind=kOutput, calls=%fused_computation.24 | convolution fusion | flops 1895563264 | bytes 30539776 | tf_op jit(solution)/shard_map/dot_general | solution.py:78
  264.6 22.2 %fusion.31 = (bf16[2048,3584]{0,1:T(8,128)(2,1)}, bf16[2048,3584]{0,1:T(8,128)(2,1)}) fusion(bf16[2048,7168]{0,1:T(8,128)(2,1)} %convert_bitcast_fusion), kind=kLoop, calls=%fused_computation.46 | loop fusion | bytes 58720256 | tf_op jit(solution)/shard_map/slice | solution.py:81
  286.8 18.6 %copy.10 = bf16[2048,3584]{1,0:T(8,128)(2,1)} copy(bf16[2048,3584]{0,1:T(8,128)(2,1)} %get-tuple-element.319) | data formatting | bytes 29360128
  305.5 18.7 %copy.11 = bf16[2048,3584]{1,0:T(8,128)(2,1)} copy(bf16[2048,3584]{0,1:T(8,128)(2,1)} %get-tuple-element.318) | data formatting | bytes 29360128
  (47 shorter events, 1.6 us)
Async XLA Ops:
  7.2 23.9 %copy-start = (bf16[64,2048]{1,0:T(8,128)(2,1)S(1)}, bf16[64,2048]{1,0:T(8,128)(2,1)}, u32[]{:S(2)}) copy-start(bf16[64,2048]{1,0:T(8,128)(2,1)} %param.9) | copy-start | bytes 786436
  7.2 101.9 %all-reduce.11.cloned.1.call-start = ((), (), s32[]{:S(2)}) async-start(), calls=%async_computation | async-start | bytes 3670016 | tf_op jit(solution)/shard_map/psum | solution.py:49
  31.0 145.3 %all-reduce.15.cloned.1.call-start = ((), (), s32[]{:S(2)}) async-start(), calls=%async_computation.2 | async-start | bytes 2097152 | tf_op jit(solution)/shard_map/psum | solution.py:53
  36.8 83.6 %copy-start.6 = (u32[32]{0:T(128)S(1)}, u32[32]{0:T(128)}, u32[]{:S(2)}) copy-start(u32[32]{0:T(128)} %constant.49) | copy-start | bytes 388
  110.8 0.8 copy-start.5
  120.3 129.0 %all-reduce.13.cloned.1.call-start = ((), (), s32[]{:S(2)}) async-start(), calls=%async_computation.1 | async-start | bytes 1835008 | tf_op jit(solution)/shard_map/psum | solution.py:76
  176.2 30.0 %copy-start.2 = (f32[64,2048]{1,0:T(8,128)S(1)}, f32[64,2048]{1,0:T(8,128)}, u32[]{:S(2)}) copy-start(f32[64,2048]{1,0:T(8,128)} %get-tuple-element.306) | copy-start | bytes 1572868
  176.2 30.0 %copy-start.3 = (f32[64,2048]{1,0:T(8,128)S(1)}, f32[64,2048]{1,0:T(8,128)}, u32[]{:S(2)}) copy-start(f32[64,2048]{1,0:T(8,128)} %get-tuple-element.307) | copy-start | bytes 1572868
  205.0 44.4 %copy-start.4 = (f32[64,7168]{1,0:T(8,128)S(1)}, f32[64,7168]{1,0:T(8,128)}, u32[]{:S(2)}) copy-start(f32[64,7168]{1,0:T(8,128)} %all-reduce.11.cloned.1.call-done) | copy-start | bytes 5505028
  305.5 18.7 %copy-start.1 = (bf16[64,2048]{1,0:T(8,128)(2,1)S(1)}, bf16[64,2048]{1,0:T(8,128)(2,1)}, u32[]{:S(2)}) copy-start(bf16[64,2048]{1,0:T(8,128)(2,1)} %param.9) | copy-start | bytes 786436
Sparse Core Ops, SparseCore 0:
  31.1 77.9 all-reduce.10
  120.5 55.7 all-reduce.14
  205.1 44.1 all-reduce.12
where the time goes:
time: 333 us; the launch traced here: 332 us
  waiting for transfers between devices  161 us (48%)
  local copies, waits for them, and re-layouts  62.4 us (19%)
  matrix products  60.5 us (18%)
  blocking collectives  22.9 us (7%)
  between operations  16.2 us (5%)
  other arithmetic  8.17 us (2%)
    psum x1, waiting for transfers between devices, local(): gate_full = lax.psum(gate_part, 'row')  72.3 us
    psum x1, waiting for transfers between devices, local(): stud_sum, teacher = lax.psum((stud_part, teach_part), 'col')  54.7 us
    unnamed x27, local copies, waits for them, and re-layouts  39.8 us
    psum x1, waiting for transfers between devices, local(): hidden_grad = lax.psum(hidden_part, 'row')  34.3 us
    slice x1, local copies, waits for them, and re-layouts, local(): both_grads[:, width_ff:]  22.2 us
    dot_general x1, matrix products, local(): lax.dot_general(tok_rows, grad_pair, (((0,), (0,)), ((), ())), preferred_...  13.6 us
    dot_general x1, matrix products, local(): gate_part = jnp.dot(tok_rows, gate_up, preferred_element_type=jnp.float32)  12.6 us
    unnamed x1, blocking collectives  11.8 us
  transfers between devices with their start and end apart: 3, of which 3 were waited for; matrix products, arithmetic and copies ran while one was open for 5% of the time, Pallas kernels for 0%

commit v1 on v0

v1 whole, which is shorter than its diff:
```python
import jax
import jax.numpy as jnp
from jax import lax
from jax.experimental import pallas as pl
from jax.experimental.pallas import tpu as pltpu
from jax.sharding import PartitionSpec as P

BF16, F32 = jnp.bfloat16, jnp.float32
MIB = 2**20


def log2(n):
    return n.bit_length() - 1


def swap(value, axis, bit):
    n = lax.axis_size(axis)
    return lax.ppermute(value, axis, [(i, i ^ (1 << bit)) for i in range(n)])


def flip_if(flag, value, axis):
    first, second = jnp.split(value, 2, axis)
    return jnp.where(flag, jnp.concatenate([second, first], axis), value)


def call(kernel, grid, in_specs, out_specs, out_shape, flops, nbytes, aliases=None, vmem=44):
    return pl.pallas_call(
        kernel,
        grid=grid,
        in_specs=in_specs,
        out_specs=out_specs,
        out_shape=out_shape,
        input_output_aliases=aliases or {},
        compiler_params=pltpu.CompilerParams(vmem_limit_bytes=vmem * MIB),
        cost_estimate=pl.CostEstimate(flops=flops, bytes_accessed=nbytes, transcendentals=0),
    )


def whole(shape):
    return pl.BlockSpec(shape, lambda *_: (0,) * len(shape))


def steps_of(width, most):
    for n in range(1, width // 128 + 1):
        if width % (128 * n) == 0 and width // n <= most:
            return n
    return 1


def halves(value, groups):
    rows, width = value.shape
    split = value.reshape(groups, 2, rows // groups // 2, width)
    return split[:, 0].reshape(rows // 2, width), split[:, 1].reshape(rows // 2, width)


def gate_up_chunk(x, w_gate, w_up, k, cw):
    rows, depth = x.shape
    half = rows // 2
    if cw % 128:
        gate = jnp.dot(x, w_gate[:, k * cw : (k + 1) * cw], preferred_element_type=F32)
        up = jnp.dot(x, w_up[:, k * cw : (k + 1) * cw], preferred_element_type=F32)
        (gate_keep, gate_send), (up_keep, up_send) = halves(gate, 2), halves(up, 2)
        return jnp.stack([gate_keep, up_keep]), jnp.stack([gate_send, up_send]).astype(BF16)
    steps = steps_of(cw, 896)
    bn = cw // steps

    def kernel(x_ref, gate_ref, up_ref, keep_ref, send_ref):
        for i, w_ref in enumerate((gate_ref, up_ref)):
            part = jnp.dot(x_ref[...], w_ref[...], preferred_element_type=F32)
            keep, send = halves(part, 2)
            keep_ref[i] = keep
            send_ref[i] = send.astype(BF16)

    wide = pl.BlockSpec((depth, bn), lambda j: (0, k * steps + j))
    out = pl.BlockSpec((2, half, bn), lambda j: (0, 0, j))
    return call(
        kernel,
        (steps,),
        [whole((rows, depth)), wide, wide],
        [out, out],
        [jax.ShapeDtypeStruct((2, half, cw), F32), jax.ShapeDtypeStruct((2, half, cw), BF16)],
        4 * rows * depth * cw,
        4 * depth * cw,
    )(x, w_gate, w_up)


def down_chunk(hidden, w_down, k, before):
    rows, cw = hidden.shape
    width = w_down.shape[1]
    half = rows // 2
    if cw % 128:
        part = jnp.dot(hidden, w_down[k * cw : (k + 1) * cw], preferred_element_type=F32)
        parts = (part[:half], part[half:])
        return parts if before is None else tuple(a + b for a, b in zip(before, parts))
    steps = steps_of(cw, 896)
    bk = cw // steps

    def kernel(h_ref, w_ref, *refs):
        keep_ref, send_ref = refs[-2:]
        j = pl.program_id(0)
        part = jnp.dot(h_ref[...], w_ref[...], preferred_element_type=F32)

        @pl.when(j == 0)
        def _():
            if before is None:
                keep_ref[...] = part[:half]
                send_ref[...] = part[half:]
            else:
                keep_ref[...] = refs[0][...] + part[:half]
                send_ref[...] = refs[1][...] + part[half:]

        @pl.when(j > 0)
        def _():
            keep_ref[...] += part[:half]
            send_ref[...] += part[half:]

    out = whole((half, width))
    shape = jax.ShapeDtypeStruct((half, width), F32)
    return call(
        kernel,
        (steps,),
        [
            pl.BlockSpec((rows, bk), lambda j: (0, j)),
            pl.BlockSpec((bk, width), lambda j: (k * steps + j, 0)),
        ]
        + ([] if before is None else [out, out]),
        [out, out],
        [shape, shape],
        2 * rows * cw * width,
        2 * cw * width,
    )(hidden, w_down, *(before or ()))


def hidden_grad_chunk(stud_grad, w_down, k, cw):
    rows, width = stud_grad.shape
    half = rows // 2
    dims = (((1,), (1,)), ((), ()))
    if cw % 128:
        part = lax.dot_general(
            stud_grad, w_down[k * cw : (k + 1) * cw], dims, preferred_element_type=F32
        )
        keep, send = halves(part, 2)
        return keep, send.astype(BF16)
    steps = steps_of(cw, 896)
    bn = cw // steps

    def kernel(g_ref, w_ref, keep_ref, send_ref):
        part = lax.dot_general(g_ref[...], w_ref[...], dims, preferred_element_type=F32)
        keep, send = halves(part, 2)
        keep_ref[...] = keep
        send_ref[...] = send.astype(BF16)

    out = pl.BlockSpec((half, bn), lambda j: (0, j))
    return call(
        kernel,
        (steps,),
        [whole((rows, width)), pl.BlockSpec((bn, width), lambda j: (k * steps + j, 0))],
        [out, out],
        [jax.ShapeDtypeStruct((half, cw), F32), jax.ShapeDtypeStruct((half, cw), BF16)],
        2 * rows * cw * width,
        2 * cw * width,
    )(stud_grad, w_down)


def outer(left, right):
    dims = (((0,), (0,)), ((), ()))
    return lax.dot_general(left, right, dims, preferred_element_type=F32).astype(BF16)


def weight_grads_chunk(x, hidden_grad, slopes, k, width_ff, before):
    rows, depth = x.shape
    cw = hidden_grad.shape[1]
    if cw % 128:
        return [outer(x, hidden_grad * slopes[i]) for i in (0, 1)]
    bm = min(512, depth)

    def kernel(x_ref, h_ref, s_ref, *refs):
        grad = h_ref[...].astype(F32)
        for i, out_ref in enumerate(refs[-2:]):
            out_ref[...] = outer(x_ref[...], (grad * s_ref[i].astype(F32)).astype(BF16))

    out = pl.BlockSpec((bm, cw), lambda i: (i, k))
    shape = jax.ShapeDtypeStruct((depth, width_ff), BF16)
    prior = [] if before is None else list(before)
    return call(
        kernel,
        (depth // bm,),
        [pl.BlockSpec((rows, bm), lambda i: (0, i)), whole((rows, cw)), whole((2, rows, cw))]
        + [pl.BlockSpec(memory_space=pl.ANY)] * len(prior),
        [out, out],
        [shape, shape],
        4 * rows * depth * cw,
        4 * depth * cw,
        {3: 0, 4: 1} if prior else None,
    )(x, hidden_grad, slopes, *prior)


def down_grad_chunk(hidden, stud_grad, k, width_ff, before):
    rows, cw = hidden.shape
    width = stud_grad.shape[1]
    if cw % 128:
        return outer(hidden, stud_grad)
    steps = steps_of(cw, 896)
    bm = cw // steps

    def kernel(h_ref, g_ref, *refs):
        refs[-1][...] = outer(h_ref[...], g_ref[...])

    prior = [] if before is None else [before]
    return call(
        kernel,
        (steps,),
        [pl.BlockSpec((rows, bm), lambda i: (0, i)), whole((rows, width))]
        + [pl.BlockSpec(memory_space=pl.ANY)] * len(prior),
        pl.BlockSpec((bm, width), lambda i: (k * steps + i, 0)),
        jax.ShapeDtypeStruct((width_ff, width), BF16),
        2 * rows * cw * width,
        2 * cw * width,
        {2: 0} if prior else None,
    )(hidden, stud_grad, *prior)


def local(student_in, teacher_hidden, proj, w_gate, w_up, w_down):
    n_row, n_col = lax.axis_size("row"), lax.axis_size("col")
    row_bits, chip_bits = log2(n_row), log2(n_col) - 1
    row_me, col_me = lax.axis_index("row"), lax.axis_index("col")
    core_me = col_me % 2 == 1
    own, width = student_in.shape
    tokens = own * n_col
    width_ff = w_gate.shape[1]
    chunks = 2 if width_ff % 256 == 0 else 1
    cw = width_ff // chunks
    twos = (2,) * chip_bits

    def row_bit(s):
        return (row_me >> s) % 2 == 1

    teach = teacher_hidden.reshape(*twos, 2, own, -1)
    for s in range(row_bits):
        teach = flip_if(row_bit(s), teach, s)
    teach = jnp.moveaxis(flip_if(core_me, teach, chip_bits), chip_bits, 0)
    teach_part = jnp.dot(teach.reshape(tokens, -1), proj, preferred_element_type=F32)

    x = student_in
    for s in reversed(range(chip_bits)):
        x = jnp.stack([x, swap(x, "col", chip_bits - s)])
    for s in range(chip_bits):
        flag = (col_me >> (chip_bits - s)) % 2 == 1
        if s < row_bits:
            flag = flag ^ row_bit(s)
        x = flip_if(flag, x, s)
    x = x.reshape(tokens // 2, width)
    x = jnp.concatenate([x, swap(x, "col", 0)])

    def reduce_rows(keep, send, lead):
        columns = keep.shape[-1]
        for s in range(row_bits):
            total = keep + swap(send, "row", s).astype(F32)
            if s < row_bits - 1:
                total = total.reshape(lead * 2, 2, -1, columns)
                keep, send = total[:, 0], total[:, 1].astype(BF16)
        return total.reshape(lead, -1, columns)

    def gather_rows(piece, lead):
        columns = piece.shape[-1]
        for s in reversed(range(row_bits)):
            piece = piece.reshape(lead, 2, 1, -1, columns)
            piece = jnp.concatenate([piece, swap(piece, "row", s)], axis=2)
        return piece.reshape(lead, tokens, columns)

    def reduce_cols(keep, send):
        total = keep + swap(send, "col", 0)
        parts = list(jnp.split(total, 2))
        for turn in range(chip_bits):
            for i, bit in enumerate((1 + turn, chip_bits - turn)):
                parts[i] = parts[i] + swap(parts[i], "col", bit)
        return jnp.concatenate(parts)

    def exchange_rows(stats):
        everything = []
        for m in range(n_row):
            if m == 0:
                everything.append(stats)
                continue
            other = lax.ppermute(stats, "row", [(i, i ^ m) for i in range(n_row)])
            other = other.reshape(*twos, own, -1)
            for s in range(row_bits):
                if (m >> s) % 2:
                    first, second = jnp.split(other, 2, s)
                    other = jnp.concatenate([second, first], s)
            everything.append(other.reshape(stats.shape))
        return everything

    def tree_sum(values):
        while len(values) > 1:
            values = [a + b for a, b in zip(values[::2], values[1::2])]
        return values[0]

    hidden, slopes_piece = [], []
    for k in range(chunks):
        keep, send = gate_up_chunk(x, w_gate, w_up, k, cw)
        total = reduce_rows(keep, send, 2)
        gate, up = total[0], total[1]
        logistic = jax.nn.sigmoid(gate)
        silu = gate * logistic
        hidden.append(gather_rows((silu * up).astype(BF16)[None], 1)[0])
        slope = logistic * (1.0 + gate * (1.0 - logistic))
        slopes_piece.append(jnp.stack([up * slope, silu]).astype(BF16))
    slopes = [gather_rows(piece, 2) for piece in slopes_piece]

    teacher = reduce_cols(teach_part[: tokens // 2], teach_part[tokens // 2 :])
    top = jnp.max(teacher, axis=1, keepdims=True)
    norm = jnp.sum(jnp.exp(teacher - top), axis=1, keepdims=True)
    stats = exchange_rows(jnp.concatenate([top, norm], axis=1))
    teach_max = stats[0][:, :1]
    for other in stats[1:]:
        teach_max = jnp.maximum(teach_max, other[:, :1])
    teach_norm = tree_sum([s[:, 1:2] * jnp.exp(s[:, :1] - teach_max) for s in stats])
    target = jnp.exp(teacher - teach_max) / teach_norm

    parts = None
    for k in range(chunks):
        parts = down_chunk(hidden[k], w_down, k, parts)
    student = x[: tokens // 2].astype(F32) + reduce_cols(*parts)
    top = jnp.max(student, axis=1, keepdims=True)
    norm = jnp.sum(jnp.exp(student - top), axis=1, keepdims=True)
    cross = jnp.sum(target * student, axis=1, keepdims=True)
    stats = exchange_rows(jnp.concatenate([top, norm, cross], axis=1))
    stud_max = stats[0][:, :1]
    for other in stats[1:]:
        stud_max = jnp.maximum(stud_max, other[:, :1])
    stud_norm = tree_sum([s[:, 1:2] * jnp.exp(s[:, :1] - stud_max) for s in stats])
    cross = tree_sum([s[:, 2:3] for s in stats])
    own_grad = (jnp.exp(student - stud_max) / stud_norm - target).astype(BF16)
    stud_grad = jnp.concatenate([own_grad, swap(own_grad, "col", 0)])

    token_loss = (stud_max + jnp.log(stud_norm) - cross).reshape(*twos, own)
    for s in range(row_bits):
        token_loss = flip_if(row_bit(s), token_loss, s)
    core_loss = jnp.sum(token_loss.reshape(1, -1), axis=1, keepdims=True)
    distill_loss = ((core_loss + swap(core_loss, "col", 0)) / tokens)[0, 0]

    hidden_grads = []
    for k in range(chunks):
        keep, send = hidden_grad_chunk(stud_grad, w_down, k, cw)
        total = reduce_rows(keep, send, 1)
        hidden_grads.append(gather_rows(total.astype(BF16), 1)[0])
    grad_down = None
    for k in range(chunks):
        grad_down = down_grad_chunk(hidden[k], stud_grad, k, width_ff, grad_down)
    grads = None
    for k in range(chunks):
        grads = weight_grads_chunk(x, hidden_grads[k], slopes[k], k, width_ff, grads)
    return (grads[0], grads[1], grad_down, distill_loss)


def solution(mesh):
    return jax.shard_map(
        local,
        mesh=mesh,
        in_specs=(
            P("col", "row"),
            P(None, "col"),
            P("col", "row"),
            P("row", "col"),
            P("row", "col"),
            P("col", "row"),
        ),
        out_specs=(P("row", "col"), P("row", "col"), P("col", "row"), P()),
        check_vma=False,
    )
```

time: 333 us -> 156 us (0.47)
  waiting for transfers between devices: 161 us -> 40.2 us
  local copies, waits for them, and re-layouts: 62.4 us -> 3.88 us
  matrix products: 60.5 us -> 4.95 us
  Pallas kernels: 0 us -> 51.9 us
  starting transfers between devices: 0.12 us -> 44.5 us
  blocking collectives: 22.9 us -> 0 us
  between operations: 16.2 us -> 3.62 us
    psum x3 -> x0, waiting for transfers between devices: 161 us -> none  [the longest x1 72.3 us: local(): gate_full = lax.psum(gate_part, 'row')]
    dot_general x6 -> x1, matrix products: 60.5 us -> 4.95 us  [local(): jnp.dot(teach.reshape(tokens, -1), proj, preferred_element_type=F32)]
    pallas_call x0 -> x10, Pallas kernels: none -> 51.9 us  [the longest x2 13.6 us: gate_up_chunk(): call(kernel, (steps,), [whole((rows, depth)), wide, wide], [out, out], [j...]
    ppermute x0 -> x41, starting transfers between devices: none -> 44.5 us  [the longest x35 36.5 us: swap(): return lax.ppermute(value, axis, [(i, i ^ 1 << bit) for i in range(n)])]
    ppermute x0 -> x41, waiting for transfers between devices: none -> 40.2 us  [the longest x35 35.2 us: swap(): return lax.ppermute(value, axis, [(i, i ^ 1 << bit) for i in range(n)])]
    unnamed x27 -> x3, local copies, waits for them, and re-layouts: 39.8 us -> 0.02 us
    slice x6 -> x1, local copies, waits for them, and re-layouts: 22.2 us -> 0.02 us  [local(): teacher = reduce_cols(teach_part[:tokens // 2], teach_part[tokens // 2:])]
    unnamed x1 -> x0, blocking collectives: 11.8 us -> none
  transfers between devices with their start and end apart: 3 -> 41, of which waited for: 3 -> 19; matrix products, arithmetic and copies ran while one was open for 5% -> 8% of each run, Pallas kernels for 0% -> 26%
where the time goes in v1:
time: 156 us
  Pallas kernels  51.9 us (33%)
  starting transfers between devices  44.5 us (29%)
  waiting for transfers between devices  40.2 us (26%)
  other arithmetic  7.07 us (5%)
  matrix products  4.95 us (3%)
  local copies, waits for them, and re-layouts  3.88 us (2%)
  between operations  3.62 us (2%)
    ppermute x35, starting transfers between devices, swap(): return lax.ppermute(value, axis, [(i, i ^ 1 << bit) for i in range(n)])  36.5 us
    ppermute x35, waiting for transfers between devices, swap(): return lax.ppermute(value, axis, [(i, i ^ 1 << bit) for i in range(n)])  35.2 us
    pallas_call x2, Pallas kernels, gate_up_chunk(): call(kernel, (steps,), [whole((rows, depth)), wide, wide], [out, out], [j...  13.6 us
    pallas_call x2, Pallas kernels, weight_grads_chunk(): call(kernel, (depth // bm,), [pl.BlockSpec((rows, bm), lambda i: (0, i)),...  12.7 us
    pallas_call x2, Pallas kernels, hidden_grad_chunk(): call(kernel, (steps,), [whole((rows, width)), pl.BlockSpec((bn, width), l...  9.09 us
    pallas_call x2, Pallas kernels, down_grad_chunk(): call(kernel, (steps,), [pl.BlockSpec((rows, bm), lambda i: (0, i)), whole...  8.45 us
    pallas_call x2, Pallas kernels, down_chunk(): call(kernel, (steps,), [pl.BlockSpec((rows, bk), lambda j: (0, j)), pl.Bl...  8.03 us
    ppermute x6, starting transfers between devices, exchange_rows(): other = lax.ppermute(stats, 'row', [(i, i ^ m) for i in range(n_row)])  8.01 us
  transfers between devices with their start and end apart: 41, of which 19 were waited for; matrix products, arithmetic and copies ran while one was open for 8% of the time, Pallas kernels for 26%

profile of v1, /device:TPU:0, one launch (start us, length us, event | category | flops | bytes accessed | tf_op | source)
XLA Modules:
  0.0 156.1 jit_solution(15908987664441098418)
XLA Ops:
  0.6 3.0 %collective-permute-start = (bf16[8,2048]{1,0:T(8,128)(2,1)}, bf16[8,2048]{1,0:T(8,128)(2,1)S(1)}, u32[]{:S(2)}, u32[]{:S(2)}) collective-permute-start(bf16[8,2048]{1,0:T(8,128)(2,1)} %param.6), channel_id=1, source_target_pairs={{0,2},{1,3},{2,0},{3,1},{4,6},{5,7},{6,4},{7,5},{8,10},{9,11},{10,... | collective-permute-start | bytes 98312 | tf_op jit(solution)/shard_map/ppermute | solution.py:18
  12.0 4.9 %fusion.39 = f32[64,2048]{1,0:T(8,128)S(1)} fusion(bf16[64,2048]{1,0:T(8,128)(2,1)S(1)} %bitcast.169, bf16[2048,2048]{1,0:T(8,128)(2,1)} %param.8), kind=kOutput, calls=%fused_computation.124 | convolution fusion | flops 536870912 | bytes 9175040 | tf_op jit(solution)/shard_map/dot_general | solution.py:242
  21.4 6.9 %shard_map.94 = (f32[2,32,1792]{2,1,0:T(8,128)S(1)}, bf16[2,32,1792]{2,1,0:T(8,128)(2,1)S(1)}) custom-call(bf16[64,2048]{1,0:T(8,128)(2,1)S(1)} %pad_maximum_fusion.2.x_ref, bf16[2048,3584]{1,0:T(8,128)(2,1)} %gate_ref.3, bf16[2048,3584]{1,0:T(8,128)(2,1)} %up_ref.3), custom_call_target="tpu_custom_call" | custom-call | flops 939524096 | bytes 14680064 | tf_op jit(solution)/shard_map/pallas_call | solution.py:76
  29.9 6.7 %shard_map.93 = (f32[2,32,1792]{2,1,0:T(8,128)S(1)}, bf16[2,32,1792]{2,1,0:T(8,128)(2,1)S(1)}) custom-call(bf16[64,2048]{1,0:T(8,128)(2,1)S(1)} %pad_maximum_fusion.2.x_ref, bf16[2048,3584]{1,0:T(8,128)(2,1)} %gate_ref.3, bf16[2048,3584]{1,0:T(8,128)(2,1)} %up_ref.3), custom_call_target="tpu_custom_call" | custom-call | flops 939524096 | bytes 14680064 | tf_op jit(solution)/shard_map/pallas_call | solution.py:76
  38.8 2.7 %collective-permute-start.8 = (bf16[4,8,1792]{2,1,0:T(8,128)(2,1)S(1)}, bf16[4,8,1792]{2,1,0:T(8,128)(2,1)S(1)}, u32[]{:S(2)}, u32[]{:S(2)}) collective-permute-start(bf16[4,8,1792]{2,1,0:T(8,128)(2,1)S(1)} %fusion.4), channel_id=1, source_target_pairs={{0,16},{8,24},{16,0},{24,8},{1,17},{9,25},{17,1},{25,9},{2,18},{10... | collective-permute-start | bytes 344072 | tf_op jit(solution)/shard_map/ppermute | solution.py:18
  41.5 4.7 %collective-permute-done.3 = bf16[2,32,1792]{2,1,0:T(8,128)(2,1)S(1)} collective-permute-done((bf16[2,32,1792]{2,1,0:T(8,128)(2,1)S(1)}, bf16[2,32,1792]{2,1,0:T(8,128)(2,1)S(1)}, u32[]{:S(2)}, u32[]{:S(2)}) %collective-permute-start.3) | collective-permute-done | bytes 229408 | tf_op jit(solution)/shard_map/ppermute | solution.py:18
  46.8 2.4 %collective-permute-start.4 = (bf16[4,8,1792]{2,1,0:T(8,128)(2,1)S(1)}, bf16[4,8,1792]{2,1,0:T(8,128)(2,1)S(1)}, u32[]{:S(2)}, u32[]{:S(2)}) collective-permute-start(bf16[4,8,1792]{2,1,0:T(8,128)(2,1)S(1)} %fusion.5), channel_id=1, source_target_pairs={{0,16},{8,24},{16,0},{24,8},{1,17},{9,25},{17,1},{25,9},{2,18},{10... | collective-permute-start | bytes 344072 | tf_op jit(solution)/shard_map/ppermute | solution.py:18
  49.8 2.8 %collective-permute-start.23 = (f32[32,2]{0,1:T(2,128)S(1)}, f32[32,2]{0,1:T(2,128)S(1)}, u32[]{:S(2)}, u32[]{:S(2)}) collective-permute-start(f32[32,2]{0,1:T(2,128)S(1)} %pad_maximum_fusion.26), channel_id=1, source_target_pairs={{0,24},{8,16},{16,8},{24,0},{1,25},{9,17},{17,9},{25,1},{2,26},{10... | collective-permute-start | bytes 776 | tf_op jit(solution)/shard_map/ppermute | solution.py:285
  56.4 2.5 %collective-permute-start.5 = (bf16[1,2,1,8,1792]{4,3,1,2,0:T(8,128)(2,1)S(1)}, bf16[1,2,1,8,1792]{4,3,1,2,0:T(8,128)(2,1)S(1)}, u32[]{:S(2)}, u32[]{:S(2)}) collective-permute-start(bf16[1,2,1,8,1792]{4,3,1,2,0:T(8,128)(2,1)S(1)} %get-tuple-element.64), channel_id=1, source_target_pairs={{0,16},{8,24},{16,0},{24,8},{1,17},{9,25},{17,1},{25,9},{2,18},{10... | collective-permute-start | bytes 172040 | tf_op jit(solution)/shard_map/ppermute | solution.py:18
  64.5 3.0 %collective-permute-done.10 = bf16[1,2,1,16,1792]{4,3,2,1,0:T(8,128)(2,1)S(1)} collective-permute-done((bf16[1,2,1,16,1792]{4,3,2,1,0:T(8,128)(2,1)S(1)}, bf16[1,2,1,16,1792]{4,3,2,1,0:T(8,128)(2,1)S(1)}, u32[]{:S(2)}, u32[]{:S(2)}) %collective-permute-start.10) | collective-permute-done | bytes 114720 | tf_op jit(solution)/shard_map/ppermute | solution.py:18
  67.5 4.0 %shard_map.95 = (f32[32,2048]{1,0:T(8,128)S(1)}, f32[32,2048]{1,0:T(8,128)S(1)}) custom-call(bf16[64,1792]{1,0:T(8,128)(2,1)S(1)} %bitcast.156, bf16[3584,2048]{1,0:T(8,128)(2,1)} %w_ref.7), custom_call_target="tpu_custom_call" | custom-call | flops 469762048 | bytes 7340032 | tf_op jit(solution)/shard_map/pallas_call | solution.py:119
  71.6 4.0 %shard_map.96 = (f32[32,2048]{1,0:T(8,128)S(1)}, f32[32,2048]{1,0:T(8,128)S(1)}) custom-call(bf16[64,1792]{1,0:T(8,128)(2,1)S(1)} %bitcast.158, bf16[3584,2048]{1,0:T(8,128)(2,1)} %w_ref.7, f32[32,2048]{1,0:T(8,128)S(1)} %get-tuple-element.24.refs_0_, f32[32,2048]{1,0:T(8,128)S(1)} %get-tuple-element.25.refs_1_), custom_call_target="tpu_custom_call" | custom-call | flops 469762048 | bytes 7340032 | tf_op jit(solution)/shard_map/pallas_call | solution.py:119
  79.4 4.5 %collective-permute-done.32 = bf16[2,2,1,8,1792]{4,3,1,2,0:T(8,128)(2,1)S(1)} collective-permute-done((bf16[2,2,1,8,1792]{4,3,1,2,0:T(8,128)(2,1)S(1)}, bf16[2,2,1,8,1792]{4,3,1,2,0:T(8,128)(2,1)S(1)}, u32[]{:S(2)}, u32[]{:S(2)}) %collective-permute-start.32) | collective-permute-done | bytes 114720 | tf_op jit(solution)/shard_map/ppermute | solution.py:18
  86.4 3.1 %collective-permute-done.13 = f32[16,2048]{1,0:T(8,128)S(1)} collective-permute-done((f32[16,2048]{1,0:T(8,128)S(1)}, f32[16,2048]{1,0:T(8,128)S(1)}, u32[]{:S(2)}, u32[]{:S(2)}) %collective-permute-start.13) | collective-permute-done | bytes 131104 | tf_op jit(solution)/shard_map/ppermute | solution.py:18
  104.1 4.5 %shard_map.98 = (f32[32,1792]{1,0:T(8,128)S(1)}, bf16[32,1792]{1,0:T(8,128)(2,1)S(1)}) custom-call(bf16[64,2048]{1,0:T(8,128)(2,1)S(1)} %pad_maximum_fusion.4.g_ref, bf16[3584,2048]{1,0:T(8,128)(2,1)} %w_ref.7), custom_call_target="tpu_custom_call" | custom-call | flops 469762048 | bytes 7340032 | tf_op jit(solution)/shard_map/pallas_call | solution.py:154
  108.7 4.5 %shard_map.97 = (f32[32,1792]{1,0:T(8,128)S(1)}, bf16[32,1792]{1,0:T(8,128)(2,1)S(1)}) custom-call(bf16[64,2048]{1,0:T(8,128)(2,1)S(1)} %pad_maximum_fusion.4.g_ref, bf16[3584,2048]{1,0:T(8,128)(2,1)} %w_ref.7), custom_call_target="tpu_custom_call" | custom-call | flops 469762048 | bytes 7340032 | tf_op jit(solution)/shard_map/pallas_call | solution.py:154
  115.3 4.2 %shard_map.101.refs_0_ = bf16[3584,2048]{1,0:T(8,128)(2,1)} custom-call(bf16[64,1792]{1,0:T(8,128)(2,1)S(1)} %bitcast.157, bf16[64,2048]{1,0:T(8,128)(2,1)S(1)} %pad_maximum_fusion.4.g_ref), custom_call_target="tpu_custom_call" | custom-call | flops 469762048 | bytes 7340032 | tf_op jit(solution)/shard_map/pallas_call | solution.py:210
  119.5 4.2 %shard_map.102 = bf16[3584,2048]{1,0:T(8,128)(2,1)} custom-call(bf16[64,1792]{1,0:T(8,128)(2,1)S(1)} %bitcast.159, bf16[64,2048]{1,0:T(8,128)(2,1)S(1)} %pad_maximum_fusion.4.g_ref, bf16[3584,2048]{1,0:T(8,128)(2,1)} %shard_map.101.refs_0_), custom_call_target="tpu_custom_call", output_to_operand_aliasing={{}: (2, {})} | custom-call | flops 469762048 | bytes 7340032 | tf_op jit(solution)/shard_map/pallas_call | solution.py:210
  124.4 2.5 %collective-permute-start.29 = (bf16[2,8,1792]{2,1,0:T(8,128)(2,1)S(1)}, bf16[2,8,1792]{2,1,0:T(8,128)(2,1)S(1)}, u32[]{:S(2)}, u32[]{:S(2)}) collective-permute-start(bf16[2,8,1792]{2,1,0:T(8,128)(2,1)S(1)} %fusion.15), channel_id=1, source_target_pairs={{0,16},{8,24},{16,0},{24,8},{1,17},{9,25},{17,1},{25,9},{2,18},{10... | collective-permute-start | bytes 172040 | tf_op jit(solution)/shard_map/ppermute | solution.py:18
  126.9 3.4 %collective-permute-done.35 = bf16[2,8,1792]{2,1,0:T(8,128)(2,1)S(1)} collective-permute-done((bf16[2,8,1792]{2,1,0:T(8,128)(2,1)S(1)}, bf16[2,8,1792]{2,1,0:T(8,128)(2,1)S(1)}, u32[]{:S(2)}, u32[]{:S(2)}) %collective-permute-start.35) | collective-permute-done | bytes 57376 | tf_op jit(solution)/shard_map/ppermute | solution.py:18
  133.4 3.1 %collective-permute-done.36 = bf16[1,2,1,8,1792]{4,3,1,2,0:T(8,128)(2,1)S(1)} collective-permute-done((bf16[1,2,1,8,1792]{4,3,1,2,0:T(8,128)(2,1)S(1)}, bf16[1,2,1,8,1792]{4,3,1,2,0:T(8,128)(2,1)S(1)}, u32[]{:S(2)}, u32[]{:S(2)}) %collective-permute-start.36) | collective-permute-done | bytes 57376 | tf_op jit(solution)/shard_map/ppermute | solution.py:18
  138.7 3.5 %collective-permute-done.37 = bf16[1,2,1,16,1792]{4,3,2,1,0:T(8,128)(2,1)S(1)} collective-permute-done((bf16[1,2,1,16,1792]{4,3,2,1,0:T(8,128)(2,1)S(1)}, bf16[1,2,1,16,1792]{4,3,2,1,0:T(8,128)(2,1)S(1)}, u32[]{:S(2)}, u32[]{:S(2)}) %collective-permute-start.37) | collective-permute-done | bytes 114720 | tf_op jit(solution)/shard_map/ppermute | solution.py:18
  142.2 6.3 %shard_map.99 = (bf16[2048,3584]{1,0:T(8,128)(2,1)}, bf16[2048,3584]{1,0:T(8,128)(2,1)}) custom-call(bf16[64,2048]{1,0:T(8,128)(2,1)S(1)} %pad_maximum_fusion.2.x_ref, bf16[64,1792]{1,0:T(8,128)(2,1)S(1)} %bitcast.163, bf16[2,64,1792]{2,1,0:T(8,128)(2,1)S(1)} %bitcast.162), custom_call_target="tpu_custom_call" | custom-call | flops 939524096 | bytes 14680064 | tf_op jit(solution)/shard_map/pallas_call | solution.py:185
  148.6 6.3 %shard_map.100 = (bf16[2048,3584]{1,0:T(8,128)(2,1)}, bf16[2048,3584]{1,0:T(8,128)(2,1)}) custom-call(bf16[64,2048]{1,0:T(8,128)(2,1)S(1)} %pad_maximum_fusion.2.x_ref, bf16[64,1792]{1,0:T(8,128)(2,1)S(1)} %bitcast.161, bf16[2,64,1792]{2,1,0:T(8,128)(2,1)S(1)} %bitcast.160, ...), custom_call_target="tpu_custom_call", output_to_operand_aliasing={{0}: (3, {}), {1}: (4, {})} | custom-call | flops 939524096 | bytes 14680064 | tf_op jit(solution)/shard_map/pallas_call | solution.py:185
  (181 shorter events, 54.4 us)
Async XLA Ops:
  0.6 6.1 %collective-permute-start = (bf16[8,2048]{1,0:T(8,128)(2,1)}, bf16[8,2048]{1,0:T(8,128)(2,1)S(1)}, u32[]{:S(2)}, u32[]{:S(2)}) collective-permute-start(bf16[8,2048]{1,0:T(8,128)(2,1)} %param.6), channel_id=1, source_target_pairs={{0,2},{1,3},{2,0},{3,1},{4,6},{5,7},{6,4},{7,5},{8,10},{9,11},{10,... | collective-permute-start | bytes 98312 | tf_op jit(solution)/shard_map/ppermute | solution.py:18
  18.7 18.4 %collective-permute-start.17 = (f32[16,2048]{1,0:T(8,128)S(1)}, f32[16,2048]{1,0:T(8,128)S(1)}, u32[]{:S(2)}, u32[]{:S(2)}) collective-permute-start(f32[16,2048]{1,0:T(8,128)S(1)} %get-tuple-element.48), channel_id=1, source_target_pairs={{0,2},{1,3},{2,0},{3,1},{4,6},{5,7},{6,4},{7,5},{8,10},{9,11},{10,... | collective-permute-start | bytes 393224 | tf_op jit(solution)/shard_map/ppermute | solution.py:18
  19.9 17.3 %collective-permute-start.19 = (f32[16,2048]{1,0:T(8,128)S(1)}, f32[16,2048]{1,0:T(8,128)S(1)}, u32[]{:S(2)}, u32[]{:S(2)}) collective-permute-start(f32[16,2048]{1,0:T(8,128)S(1)} %get-tuple-element.49), channel_id=1, source_target_pairs={{0,4},{1,5},{2,6},{3,7},{4,0},{5,1},{6,2},{7,3},{8,12},{9,13},{10,... | collective-permute-start | bytes 393224 | tf_op jit(solution)/shard_map/ppermute | solution.py:18
  28.3 10.5 %collective-permute-start.7 = (bf16[2,32,1792]{2,1,0:T(8,128)(2,1)S(1)}, bf16[2,32,1792]{2,1,0:T(8,128)(2,1)S(1)}, u32[]{:S(2)}, u32[]{:S(2)}) collective-permute-start(bf16[2,32,1792]{2,1,0:T(8,128)(2,1)S(1)} %get-tuple-element.23), channel_id=1, source_target_pairs={{0,8},{8,0},{16,24},{24,16},{1,9},{9,1},{17,25},{25,17},{2,10},{10... | collective-permute-start | bytes 688136 | tf_op jit(solution)/shard_map/ppermute | solution.py:18
  36.7 9.5 %collective-permute-start.3 = (bf16[2,32,1792]{2,1,0:T(8,128)(2,1)S(1)}, bf16[2,32,1792]{2,1,0:T(8,128)(2,1)S(1)}, u32[]{:S(2)}, u32[]{:S(2)}) collective-permute-start(bf16[2,32,1792]{2,1,0:T(8,128)(2,1)S(1)} %get-tuple-element.21), channel_id=1, source_target_pairs={{0,8},{8,0},{16,24},{24,16},{1,9},{9,1},{17,25},{25,17},{2,10},{10... | collective-permute-start | bytes 688136 | tf_op jit(solution)/shard_map/ppermute | solution.py:18
  37.2 9.0 %collective-permute-start.18 = (f32[16,2048]{1,0:T(8,128)S(1)}, f32[16,2048]{1,0:T(8,128)S(1)}, u32[]{:S(2)}, u32[]{:S(2)}) collective-permute-start(f32[16,2048]{1,0:T(8,128)S(1)} %get-tuple-element.46), channel_id=1, source_target_pairs={{0,4},{1,5},{2,6},{3,7},{4,0},{5,1},{6,2},{7,3},{8,12},{9,13},{10,... | collective-permute-start | bytes 393224 | tf_op jit(solution)/shard_map/ppermute | solution.py:18
  37.8 8.5 %collective-permute-start.20 = (f32[16,2048]{1,0:T(8,128)S(1)}, f32[16,2048]{1,0:T(8,128)S(1)}, u32[]{:S(2)}, u32[]{:S(2)}) collective-permute-start(f32[16,2048]{1,0:T(8,128)S(1)} %get-tuple-element.47), channel_id=1, source_target_pairs={{0,2},{1,3},{2,0},{3,1},{4,6},{5,7},{6,4},{7,5},{8,10},{9,11},{10,... | collective-permute-start | bytes 393224 | tf_op jit(solution)/shard_map/ppermute | solution.py:18
  38.8 16.7 %collective-permute-start.8 = (bf16[4,8,1792]{2,1,0:T(8,128)(2,1)S(1)}, bf16[4,8,1792]{2,1,0:T(8,128)(2,1)S(1)}, u32[]{:S(2)}, u32[]{:S(2)}) collective-permute-start(bf16[4,8,1792]{2,1,0:T(8,128)(2,1)S(1)} %fusion.4), channel_id=1, source_target_pairs={{0,16},{8,24},{16,0},{24,8},{1,17},{9,25},{17,1},{25,9},{2,18},{10... | collective-permute-start | bytes 344072 | tf_op jit(solution)/shard_map/ppermute | solution.py:18
  46.8 9.5 %collective-permute-start.4 = (bf16[4,8,1792]{2,1,0:T(8,128)(2,1)S(1)}, bf16[4,8,1792]{2,1,0:T(8,128)(2,1)S(1)}, u32[]{:S(2)}, u32[]{:S(2)}) collective-permute-start(bf16[4,8,1792]{2,1,0:T(8,128)(2,1)S(1)} %fusion.5), channel_id=1, source_target_pairs={{0,16},{8,24},{16,0},{24,8},{1,17},{9,25},{17,1},{25,9},{2,18},{10... | collective-permute-start | bytes 344072 | tf_op jit(solution)/shard_map/ppermute | solution.py:18
  55.7 5.9 %collective-permute-start.9 = (bf16[1,2,1,8,1792]{4,3,1,2,0:T(8,128)(2,1)S(1)}, bf16[1,2,1,8,1792]{4,3,1,2,0:T(8,128)(2,1)S(1)}, u32[]{:S(2)}, u32[]{:S(2)}) collective-permute-start(bf16[1,2,1,8,1792]{4,3,1,2,0:T(8,128)(2,1)S(1)} %get-tuple-element.61), channel_id=1, source_target_pairs={{0,16},{8,24},{16,0},{24,8},{1,17},{9,25},{17,1},{25,9},{2,18},{10... | collective-permute-start | bytes 172040 | tf_op jit(solution)/shard_map/ppermute | solution.py:18
  56.4 6.0 %collective-permute-start.5 = (bf16[1,2,1,8,1792]{4,3,1,2,0:T(8,128)(2,1)S(1)}, bf16[1,2,1,8,1792]{4,3,1,2,0:T(8,128)(2,1)S(1)}, u32[]{:S(2)}, u32[]{:S(2)}) collective-permute-start(bf16[1,2,1,8,1792]{4,3,1,2,0:T(8,128)(2,1)S(1)} %get-tuple-element.64), channel_id=1, source_target_pairs={{0,16},{8,24},{16,0},{24,8},{1,17},{9,25},{17,1},{25,9},{2,18},{10... | collective-permute-start | bytes 172040 | tf_op jit(solution)/shard_map/ppermute | solution.py:18
  58.9 16.9 %collective-permute-start.38 = (bf16[2,2,1,8,1792]{4,3,1,2,0:T(8,128)(2,1)S(1)}, bf16[2,2,1,8,1792]{4,3,1,2,0:T(8,128)(2,1)S(1)}, u32[]{:S(2)}, u32[]{:S(2)}) collective-permute-start(bf16[2,2,1,8,1792]{4,3,1,2,0:T(8,128)(2,1)S(1)} %pad_maximum_fusion.16), channel_id=1, source_target_pairs={{0,16},{8,24},{16,0},{24,8},{1,17},{9,25},{17,1},{25,9},{2,18},{10... | collective-permute-start | bytes 344072 | tf_op jit(solution)/shard_map/ppermute | solution.py:18
  62.4 9.1 %collective-permute-start.6 = (bf16[1,2,1,16,1792]{4,3,2,1,0:T(8,128)(2,1)S(1)}, bf16[1,2,1,16,1792]{4,3,2,1,0:T(8,128)(2,1)S(1)}, u32[]{:S(2)}, u32[]{:S(2)}) collective-permute-start(bf16[1,2,1,16,1792]{4,3,2,1,0:T(8,128)(2,1)S(1)} %copy_bitcast_fusion.6), channel_id=1, source_target_pairs={{0,8},{8,0},{16,24},{24,16},{1,9},{9,1},{17,25},{25,17},{2,10},{10... | collective-permute-start | bytes 344072 | tf_op jit(solution)/shard_map/ppermute | solution.py:18
  75.7 8.2 %collective-permute-start.32 = (bf16[2,2,1,8,1792]{4,3,1,2,0:T(8,128)(2,1)S(1)}, bf16[2,2,1,8,1792]{4,3,1,2,0:T(8,128)(2,1)S(1)}, u32[]{:S(2)}, u32[]{:S(2)}) collective-permute-start(bf16[2,2,1,8,1792]{4,3,1,2,0:T(8,128)(2,1)S(1)} %pad_maximum_fusion.14), channel_id=1, source_target_pairs={{0,16},{8,24},{16,0},{24,8},{1,17},{9,25},{17,1},{25,9},{2,18},{10... | collective-permute-start | bytes 344072 | tf_op jit(solution)/shard_map/ppermute | solution.py:18
  75.8 10.5 %collective-permute-start.39 = (bf16[2,2,1,16,1792]{4,3,2,1,0:T(8,128)(2,1)S(1)}, bf16[2,2,1,16,1792]{4,3,2,1,0:T(8,128)(2,1)S(1)}, u32[]{:S(2)}, u32[]{:S(2)}) collective-permute-start(bf16[2,2,1,16,1792]{4,3,2,1,0:T(8,128)(2,1)S(1)} %copy_bitcast_fusion.1), channel_id=1, source_target_pairs={{0,8},{8,0},{16,24},{24,16},{1,9},{9,1},{17,25},{25,17},{2,10},{10... | collective-permute-start | bytes 688136 | tf_op jit(solution)/shard_map/ppermute | solution.py:18
  77.7 6.3 %collective-permute-start.12 = (f32[16,2048]{1,0:T(8,128)S(1)}, f32[16,2048]{1,0:T(8,128)S(1)}, u32[]{:S(2)}, u32[]{:S(2)}) collective-permute-start(f32[16,2048]{1,0:T(8,128)S(1)} %get-tuple-element.58), channel_id=1, source_target_pairs={{0,2},{1,3},{2,0},{3,1},{4,6},{5,7},{6,4},{7,5},{8,10},{9,11},{10,... | collective-permute-start | bytes 393224 | tf_op jit(solution)/shard_map/ppermute | solution.py:18
  83.9 8.2 %collective-permute-start.33 = (bf16[2,2,1,16,1792]{4,3,2,1,0:T(8,128)(2,1)S(1)}, bf16[2,2,1,16,1792]{4,3,2,1,0:T(8,128)(2,1)S(1)}, u32[]{:S(2)}, u32[]{:S(2)}) collective-permute-start(bf16[2,2,1,16,1792]{4,3,2,1,0:T(8,128)(2,1)S(1)} %copy_bitcast_fusion.2), channel_id=1, source_target_pairs={{0,8},{8,0},{16,24},{24,16},{1,9},{9,1},{17,25},{25,17},{2,10},{10... | collective-permute-start | bytes 688136 | tf_op jit(solution)/shard_map/ppermute | solution.py:18
  108.6 15.2 %collective-permute-start.34 = (bf16[32,1792]{1,0:T(8,128)(2,1)S(1)}, bf16[32,1792]{1,0:T(8,128)(2,1)S(1)}, u32[]{:S(2)}, u32[]{:S(2)}) collective-permute-start(bf16[32,1792]{1,0:T(8,128)(2,1)S(1)} %get-tuple-element.31), channel_id=1, source_target_pairs={{0,8},{8,0},{16,24},{24,16},{1,9},{9,1},{17,25},{25,17},{2,10},{10... | collective-permute-start | bytes 344072 | tf_op jit(solution)/shard_map/ppermute | solution.py:18
  113.3 11.1 %collective-permute-start.28 = (bf16[32,1792]{1,0:T(8,128)(2,1)S(1)}, bf16[32,1792]{1,0:T(8,128)(2,1)S(1)}, u32[]{:S(2)}, u32[]{:S(2)}) collective-permute-start(bf16[32,1792]{1,0:T(8,128)(2,1)S(1)} %get-tuple-element.29), channel_id=1, source_target_pairs={{0,8},{8,0},{16,24},{24,16},{1,9},{9,1},{17,25},{25,17},{2,10},{10... | collective-permute-start | bytes 344072 | tf_op jit(solution)/shard_map/ppermute | solution.py:18
  123.8 6.5 %collective-permute-start.35 = (bf16[2,8,1792]{2,1,0:T(8,128)(2,1)S(1)}, bf16[2,8,1792]{2,1,0:T(8,128)(2,1)S(1)}, u32[]{:S(2)}, u32[]{:S(2)}) collective-permute-start(bf16[2,8,1792]{2,1,0:T(8,128)(2,1)S(1)} %fusion.17), channel_id=1, source_target_pairs={{0,16},{8,24},{16,0},{24,8},{1,17},{9,25},{17,1},{25,9},{2,18},{10... | collective-permute-start | bytes 172040 | tf_op jit(solution)/shard_map/ppermute | solution.py:18
  124.4 7.4 %collective-permute-start.29 = (bf16[2,8,1792]{2,1,0:T(8,128)(2,1)S(1)}, bf16[2,8,1792]{2,1,0:T(8,128)(2,1)S(1)}, u32[]{:S(2)}, u32[]{:S(2)}) collective-permute-start(bf16[2,8,1792]{2,1,0:T(8,128)(2,1)S(1)} %fusion.15), channel_id=1, source_target_pairs={{0,16},{8,24},{16,0},{24,8},{1,17},{9,25},{17,1},{25,9},{2,18},{10... | collective-permute-start | bytes 172040 | tf_op jit(solution)/shard_map/ppermute | solution.py:18
  130.3 6.2 %collective-permute-start.36 = (bf16[1,2,1,8,1792]{4,3,1,2,0:T(8,128)(2,1)S(1)}, bf16[1,2,1,8,1792]{4,3,1,2,0:T(8,128)(2,1)S(1)}, u32[]{:S(2)}, u32[]{:S(2)}) collective-permute-start(bf16[1,2,1,8,1792]{4,3,1,2,0:T(8,128)(2,1)S(1)} %fusion.16), channel_id=1, source_target_pairs={{0,16},{8,24},{16,0},{24,8},{1,17},{9,25},{17,1},{25,9},{2,18},{10... | collective-permute-start | bytes 172040 | tf_op jit(solution)/shard_map/ppermute | solution.py:18
  131.8 6.0 %collective-permute-start.30 = (bf16[1,2,1,8,1792]{4,3,1,2,0:T(8,128)(2,1)S(1)}, bf16[1,2,1,8,1792]{4,3,1,2,0:T(8,128)(2,1)S(1)}, u32[]{:S(2)}, u32[]{:S(2)}) collective-permute-start(bf16[1,2,1,8,1792]{4,3,1,2,0:T(8,128)(2,1)S(1)} %fusion.14), channel_id=1, source_target_pairs={{0,16},{8,24},{16,0},{24,8},{1,17},{9,25},{17,1},{25,9},{2,18},{10... | collective-permute-start | bytes 172040 | tf_op jit(solution)/shard_map/ppermute | solution.py:18
  137.8 10.8 %collective-permute-start.31 = (bf16[1,2,1,16,1792]{4,3,2,1,0:T(8,128)(2,1)S(1)}, bf16[1,2,1,16,1792]{4,3,2,1,0:T(8,128)(2,1)S(1)}, u32[]{:S(2)}, u32[]{:S(2)}) collective-permute-start(bf16[1,2,1,16,1792]{4,3,2,1,0:T(8,128)(2,1)S(1)} %copy_bitcast_fusion.4), channel_id=1, source_target_pairs={{0,8},{8,0},{16,24},{24,16},{1,9},{9,1},{17,25},{25,17},{2,10},{10... | collective-permute-start | bytes 344072 | tf_op jit(solution)/shard_map/ppermute | solution.py:18
  (17 other events, 77.2 us)

commit v2 on v0

v2 whole, which is shorter than its diff:
```python
import jax
import jax.numpy as jnp
from jax import lax
from jax.experimental import pallas as pl
from jax.experimental.pallas import tpu as pltpu
from jax.sharding import PartitionSpec as P

BF16, F32 = jnp.bfloat16, jnp.float32
MIB = 2**20


def log2(n):
    return n.bit_length() - 1


def swap(value, axis, mask):
    return lax.ppermute(value, axis, [(i, i ^ mask) for i in range(lax.axis_size(axis))])


def after(value, others):
    return lax.optimization_barrier((value, others))[0] if jax.tree.leaves(others) else value


VMEM = pl.BlockSpec(memory_space=pltpu.VMEM)


def in_hbm(array):
    return pltpu.with_memory_space_constraint(array, pltpu.HBM)


def spans(start, stop):
    first = min(256, stop - start)
    n = -(-(stop - start - first) // 896)
    cuts = [start, *(start + first + (stop - start - first) * i // (128 * max(n, 1)) * 128 for i in range(n)), stop]
    return list(zip(cuts[:-1], cuts[1:])) if n else [(start, stop)]


def streamed(x, weights, pieces, product, out_shapes, store):
    n = len(pieces)
    shapes = [tuple(cut.stop - cut.start for cut in cuts) for _, cuts in pieces]

    def kernel(x_ref, *refs):
        w_refs, refs = refs[: len(weights)], refs[len(weights) :]
        out_refs, buffers, semaphores = refs[: len(out_shapes)], refs[len(out_shapes) : -1], refs[-1]
        copies = [
            pltpu.make_async_copy(w_refs[which].at[cuts], buffer, semaphores.at[i])
            for i, ((which, cuts), buffer) in enumerate(zip(pieces, buffers))
        ]
        for copy in copies:
            copy.start()
        for i, copy in enumerate(copies):
            copy.wait()
            store(out_refs, i, product(x_ref[...], buffers[i][...]))

    size = sum(a * b for a, b in shapes)
    return pl.pallas_call(
        kernel,
        in_specs=[VMEM] + [pl.BlockSpec(memory_space=pltpu.HBM)] * len(weights),
        out_specs=[VMEM] * len(out_shapes),
        out_shape=out_shapes,
        scratch_shapes=[pltpu.VMEM(shape, BF16) for shape in shapes]
        + [pltpu.SemaphoreType.DMA((n,))],
        compiler_params=pltpu.CompilerParams(vmem_limit_bytes=2 * size + 8 * MIB),
        cost_estimate=pl.CostEstimate(
            flops=2 * x.shape[0] * size, bytes_accessed=2 * size, transcendentals=0
        ),
    )(x, *[in_hbm(w) for w in weights])


def products(x, *weights):
    depth, width = weights[0].shape
    if width % 128:
        return [jnp.dot(x, w, preferred_element_type=F32) for w in weights]
    pieces = []
    for which in range(len(weights)):
        cuts = spans(0, width) if which == 0 else [(at, at + 896) for at in range(0, width, 896)]
        pieces += [(which, (slice(0, depth), slice(at, min(to, width)))) for at, to in cuts]

    def product(left, piece):
        return jnp.dot(left, piece, preferred_element_type=F32)

    def store(refs, n, part):
        which, (_, columns) = pieces[n]
        refs[which][:, columns] = part

    shape = jax.ShapeDtypeStruct((x.shape[0], width), F32)
    return streamed(x, weights, pieces, product, [shape] * len(weights), store)


def fetched(array, tie):
    def kernel(in_ref, out_ref, semaphore):
        copy = pltpu.make_async_copy(in_ref, out_ref, semaphore)
        copy.start()
        copy.wait()

    return pl.pallas_call(
        kernel,
        in_specs=[pl.BlockSpec(memory_space=pltpu.HBM)],
        out_specs=VMEM,
        out_shape=pltpu.VMEM(array.shape, array.dtype),
        scratch_shapes=[pltpu.SemaphoreType.DMA],
        compiler_params=pltpu.CompilerParams(vmem_limit_bytes=20 * MIB),
        cost_estimate=pl.CostEstimate(flops=0, bytes_accessed=2 * array.size, transcendentals=0),
    )(after(array, tie))


def call(kernel, grid, in_specs, out_specs, out_shape, flops, nbytes, aliases=None, vmem=44):
    return pl.pallas_call(
        kernel,
        grid=grid,
        in_specs=in_specs,
        out_specs=out_specs,
        out_shape=out_shape,
        input_output_aliases=aliases or {},
        compiler_params=pltpu.CompilerParams(vmem_limit_bytes=vmem * MIB),
        cost_estimate=pl.CostEstimate(flops=flops, bytes_accessed=nbytes, transcendentals=0),
    )


def whole(array):
    return pl.BlockSpec(array.shape, lambda *_: (0,) * len(array.shape))


def steps_of(width, most):
    for n in range(1, width // 128 + 1):
        if width % (128 * n) == 0 and width // n <= most:
            return n
    return 1


def halves(value, groups):
    rows, width = value.shape
    split = value.reshape(groups, 2, rows // groups // 2, width)
    return split[:, 0].reshape(rows // 2, width), split[:, 1].reshape(rows // 2, width)


def joined(refs):
    return jnp.concatenate([ref[...] for ref in refs])


def outer(left, right):
    dims = (((0,), (0,)), ((), ()))
    return lax.dot_general(left, right, dims, preferred_element_type=F32).astype(BF16)


def down_product(hidden, w_down, groups):
    depth, width = w_down.shape
    rows = sum(piece.shape[0] for piece in hidden)
    if depth % 128:
        return halves(jnp.dot(jnp.concatenate(hidden), w_down, preferred_element_type=F32), groups)
    bn = width // steps_of(width, 512)
    n = len(hidden)

    def kernel(*refs):
        w_ref, out_refs = refs[n], refs[n + 1 :]
        left = joined(refs[:n])
        for at in range(0, width, bn):
            part = jnp.dot(left, w_ref[:, at : at + bn], preferred_element_type=F32)
            for out_ref, half in zip(out_refs, halves(part, groups)):
                out_ref[:, at : at + bn] = half

    shape = jax.ShapeDtypeStruct((rows // 2, width), F32)
    return call(
        kernel,
        (),
        [VMEM] * (n + 1),
        [VMEM] * 2,
        [shape] * 2,
        2 * rows * depth * width,
        2 * depth * width,
        vmem=20,
    )(*hidden, pltpu.with_memory_space_constraint(w_down, pltpu.VMEM))


def hidden_grad_chunk(stud_grad, w_down, k, cw):
    rows, width = stud_grad.shape
    half = rows // 2
    dims = (((1,), (1,)), ((), ()))
    if cw % 128:
        rows_k = w_down[k * cw : (k + 1) * cw]
        part = lax.dot_general(stud_grad, rows_k, dims, preferred_element_type=F32)
        return part[:half], part[half:].astype(BF16)
    start = k * cw
    pieces = [(0, (slice(at, to), slice(0, width))) for at, to in spans(start, start + cw)]

    def product(left, piece):
        return lax.dot_general(left, piece, dims, preferred_element_type=F32)

    def store(refs, n, part):
        rows_n = pieces[n][1][0]
        columns = slice(rows_n.start - start, rows_n.stop - start)
        refs[0][:, columns] = part[:half]
        refs[1][:, columns] = part[half:].astype(BF16)

    shapes = [jax.ShapeDtypeStruct((half, cw), F32), jax.ShapeDtypeStruct((half, cw), BF16)]
    return streamed(stud_grad, [w_down], pieces, product, shapes, store)


def weight_grads_chunk(x, hidden_grad, slopes, k, cw, before):
    rows, depth = x.shape
    width_ff = slopes.shape[2]
    if cw % 128:
        return [outer(x, hidden_grad * slopes[i, :, k * cw : (k + 1) * cw]) for i in (0, 1)]
    bm = min(512, depth)

    def kernel(x_ref, h_ref, s_ref, *refs):
        grad = h_ref[...].astype(F32)
        for i, out_ref in enumerate(refs[-2:]):
            out_ref[...] = outer(x_ref[...], (grad * s_ref[i].astype(F32)).astype(BF16))

    out = pl.BlockSpec((bm, cw), lambda i: (i, k))
    shape = jax.ShapeDtypeStruct((depth, width_ff), BF16)
    prior = [] if before is None else list(before)
    return call(
        kernel,
        (depth // bm,),
        [
            pl.BlockSpec((rows, bm), lambda i: (0, i)),
            whole(hidden_grad),
            pl.BlockSpec((2, rows, cw), lambda i: (0, 0, k)),
        ]
        + [pl.BlockSpec(memory_space=pl.ANY)] * len(prior),
        [out, out],
        [shape, shape],
        4 * rows * depth * cw,
        4 * depth * cw,
        {3: 0, 4: 1} if prior else None,
    )(x, hidden_grad, slopes, *prior)


def down_grad_part(hidden, stud_grad, k, parts, before):
    n, (rows, width) = len(hidden), stud_grad.shape
    width_ff = hidden[0].shape[1]
    if width_ff % 128:
        return outer(jnp.concatenate(hidden), stud_grad)
    bm = width_ff // steps_of(width_ff, 896)
    steps = width_ff // bm // parts

    def kernel(*refs):
        refs[-1][...] = outer(joined(refs[:n]), refs[n][...])

    prior = [] if before is None else [before]
    return call(
        kernel,
        (steps,),
        [pl.BlockSpec((piece.shape[0], bm), lambda i: (0, k * steps + i)) for piece in hidden]
        + [whole(stud_grad)]
        + [pl.BlockSpec(memory_space=pl.ANY)] * len(prior),
        pl.BlockSpec((bm, width), lambda i: (k * steps + i, 0)),
        jax.ShapeDtypeStruct((width_ff, width), BF16),
        2 * rows * width_ff * width // parts,
        2 * width_ff * width // parts,
        {n + 1: 0} if prior else None,
    )(*hidden, stud_grad, *prior)


def local(student_in, teacher_hidden, proj, w_gate, w_up, w_down):
    n_row, n_col = lax.axis_size("row"), lax.axis_size("col")
    n_chip = n_col // 2
    rest = n_chip // n_row
    row_bits, chip_bits = log2(n_row), log2(n_chip)
    row_me, col_me = lax.axis_index("row"), lax.axis_index("col")
    chip_me, core_me = col_me // 2, col_me % 2
    own, width = student_in.shape
    tokens = own * n_col
    width_ff = w_gate.shape[1]
    chunks = 2 if width_ff % 256 == 0 else 1
    cw = width_ff // chunks

    def turned(m):
        return sum(((m >> s) % 2) << (row_bits - 1 - s) for s in range(row_bits))

    def mask(m):
        return turned(m) * rest

    def reorder(rows, chip_mask, core_mask):
        at = jnp.arange(tokens)
        source = (((at // own) ^ (chip_mask * 2 + core_mask)) * own) + at % own
        pick = (source[:, None] == jnp.arange(tokens)[None, :]).astype(BF16)
        return jnp.dot(pick, rows, preferred_element_type=F32).astype(BF16)

    def tree_sum(values):
        while len(values) > 1:
            values = [a + b for a, b in zip(values[::2], values[1::2])]
        return values[0]

    def to_rows(pieces):
        return [swap(pieces[m], "row", m) for m in range(1, n_row)]

    def beside(moved, work):
        return lax.optimization_barrier((moved, work))

    def row_sum(keep, arrived):
        total = keep
        for part in arrived:
            total = total + part.astype(F32)
        return total

    def chip_sum(parts, turn):
        bits = (1 + turn, chip_bits - turn)
        return [part + swap(part, "col", 1 << bit) for part, bit in zip(parts, bits)]

    teacher = reorder(teacher_hidden, mask(row_me), core_me)
    x = student_in
    for s in reversed(range(chip_bits)):
        x, teacher = beside(jnp.stack([x, swap(x, "col", 2 << (chip_bits - 1 - s))]), teacher)
        if s == chip_bits - 1:
            teacher = products(teacher, proj)[0]
    for s in range(chip_bits):
        flag = (chip_me >> (chip_bits - 1 - s)) % 2 == 1
        if s < row_bits:
            flag = flag ^ ((row_me >> s) % 2 == 1)
        first, second = jnp.split(x, 2, s)
        x = jnp.where(flag, jnp.concatenate([second, first], s), x)
    x = x.reshape(n_chip, 1, own, width)
    x = jnp.concatenate([x, swap(x, "col", 1)], axis=1).reshape(tokens, width)
    teacher = halves(teacher, n_chip)
    teacher = teacher[0] + swap(teacher[1], "col", 1)
    x, teacher = beside(x, teacher)

    q = tokens // n_row
    teacher = teacher + swap(teacher, "col", 2)
    both = products(x, w_gate, w_up)
    both, teacher = beside(both, teacher)
    pieces = []
    for m in range(n_row):
        at = turned(m) * q
        pieces.append(jnp.stack([part[at : at + q] for part in both]))
    send = [piece.astype(BF16) for piece in pieces]
    near = fetched(w_down, send[1:]) if width_ff % 128 == 0 else w_down
    arrived, near = beside(to_rows(send), near)
    gate, up = row_sum(pieces[0], arrived)
    logistic = jax.nn.sigmoid(gate)
    silu = gate * logistic
    slope = logistic * (1.0 + gate * (1.0 - logistic))
    slopes = jnp.stack([up * slope, silu]).astype(BF16)
    piece = (silu * up).astype(BF16)
    arrived = to_rows([piece] * n_row)
    teacher = after(teacher, piece)
    for s in range(1, chip_bits):
        teacher = teacher + swap(teacher, "col", 2 << s)
    arrived, teacher = beside(arrived, teacher)
    hidden = [[piece, *arrived][turned(m)] for m in range(n_row)]

    parts = down_product(hidden, near, n_chip)
    parts = jnp.split(parts[0] + swap(parts[1], "col", 1), 2)
    for turn in range(chip_bits):
        parts = chip_sum(parts, turn)
    student = x.reshape(n_chip, 2, own, width)[:, 0].reshape(tokens // 2, width).astype(F32)
    student = student + jnp.concatenate(parts)
    slopes = after(slopes, hidden)
    for s in reversed(range(1, row_bits)):
        slopes = jnp.concatenate([slopes, swap(slopes, "row", 1 << s)], axis=1)
    student, slopes = beside(student, slopes)
    teach_top = jnp.max(teacher, axis=1, keepdims=True)
    teach_exp = jnp.exp(teacher - teach_top)
    teach_norm = jnp.sum(teach_exp, axis=1, keepdims=True)

    top = jnp.max(student, axis=1, keepdims=True)
    stud_exp = jnp.exp(student - top)
    norm = jnp.sum(stud_exp, axis=1, keepdims=True)
    cross = jnp.sum(teach_exp * student, axis=1, keepdims=True)
    own_stats = jnp.concatenate([top, norm, teach_top, teach_norm, cross], axis=1)
    stats = [own_stats]
    for m, other in enumerate(to_rows([own_stats] * n_row), 1):
        other = other.reshape(n_chip, own, -1)
        other = jnp.concatenate([other[j ^ mask(m)] for j in range(n_chip)])
        stats.append(other)

    def merged_max(i):
        most = stats[0][:, i : i + 1]
        for other in stats[1:]:
            most = jnp.maximum(most, other[:, i : i + 1])
        return most, [jnp.exp(s[:, i : i + 1] - most) for s in stats]

    def merged_sum(i, scales):
        return tree_sum([s[:, i : i + 1] * scale for s, scale in zip(stats, scales)])

    stud_max, stud_scales = merged_max(0)
    stud_norm = merged_sum(1, stud_scales)
    _, teach_scales = merged_max(2)
    teach_norm = merged_sum(3, teach_scales)
    cross = merged_sum(4, teach_scales) / teach_norm
    own_grad = stud_exp * (stud_scales[0] / stud_norm) - teach_exp * (teach_scales[0] / teach_norm)
    own_grad = own_grad.astype(BF16)
    pair = [v.reshape(n_chip, 1, own, width) for v in (own_grad, swap(own_grad, "col", 1))]
    stud_grad = jnp.concatenate(pair, axis=1).reshape(tokens, width)

    token_loss = stud_max + jnp.log(stud_norm) - cross
    core_loss = tree_sum([token_loss[j * own : (j + 1) * own] for j in range(n_chip)])
    core_loss = jnp.sum(core_loss, axis=0, keepdims=True)

    last_slopes = swap(after(slopes, own_grad), "row", 1)
    transfers = 2 * row_bits - 1
    keep, send, grad_down, grads, loss = [None] * chunks, [None] * chunks, None, None, core_loss
    for t in range(chunks + transfers):
        active = {k: t - 1 - k for k in range(chunks) if 0 <= t - 1 - k < transfers}
        moved = {k: swap(send[k], "row", 1 << min(i, transfers - 1 - i)) for k, i in active.items()}
        tie = [send[k] for k in active]
        made = {}
        if t < chunks:
            made["parts"] = hidden_grad_chunk(after(stud_grad, tie), w_down, t, cw)
        if t == 1:
            made["slopes"] = jnp.concatenate([slopes, last_slopes], axis=1)
        if 0 <= t - chunks < chunks:
            k = t - chunks
            made["grad_down"] = down_grad_part(after(hidden, tie), stud_grad, k, chunks, grad_down)
        if t == chunks:
            made["loss"] = loss + swap(after(loss, tie), "col", 1)
        if t == chunks + transfers - 1 and chunks > 1:
            made["grads"] = weight_grads_chunk(x, after(send[0], tie), slopes, 0, cw, None)
        moved, made = lax.optimization_barrier((moved, made))
        if "parts" in made:
            keep[t], send[t] = made["parts"]
        slopes, loss = made.get("slopes", slopes), made.get("loss", loss)
        grad_down, grads = made.get("grad_down", grad_down), made.get("grads", grads)
        for k, i in active.items():
            if i < row_bits:
                total = keep[k] + moved[k].astype(F32)
                if i < row_bits - 2:
                    keep[k], send[k] = total[: total.shape[0] // 2], total[total.shape[0] // 2 :].astype(BF16)
                elif i == row_bits - 2:
                    first, second = jnp.split(total.astype(BF16), 2)
                    keep[k], send[k] = total, jnp.concatenate([second, first])
                else:
                    send[k] = total.astype(BF16)
            else:
                send[k] = jnp.concatenate([send[k], moved[k]])
    for k in range(0 if grads is None else 1, chunks):
        grads = weight_grads_chunk(x, send[k], slopes, k, cw, grads)
    return grads[0], grads[1], grad_down, loss[0, 0] / tokens


def solution(mesh):
    return jax.shard_map(
        local,
        mesh=mesh,
        in_specs=(
            P("col", "row"),
            P(None, "col"),
            P("col", "row"),
            P("row", "col"),
            P("row", "col"),
            P("col", "row"),
        ),
        out_specs=(P("row", "col"), P("row", "col"), P("col", "row"), P()),
        check_vma=False,
    )
```

time: 333 us -> 136 us (0.41)
  waiting for transfers between devices: 161 us -> 41.5 us
  local copies, waits for them, and re-layouts: 62.4 us -> 0.43 us
  matrix products: 60.5 us -> 0.26 us
  Pallas kernels: 0 us -> 50.2 us
  starting transfers between devices: 0.12 us -> 35.9 us
  blocking collectives: 22.9 us -> 0 us
  between operations: 16.2 us -> 3.52 us
  other arithmetic: 8.17 us -> 3.52 us
    psum x3 -> x0, waiting for transfers between devices: 161 us -> none  [the longest x1 72.3 us: local(): gate_full = lax.psum(gate_part, 'row')]
    dot_general x6 -> x1, matrix products: 60.5 us -> 0.26 us  [reorder(): return jnp.dot(pick, rows, preferred_element_type=F32).astype(BF16)]
    pallas_call x0 -> x10, Pallas kernels: none -> 50.2 us  [the longest x4 25.2 us: streamed(): pl.pallas_call(kernel, in_specs=[VMEM] + [pl.BlockSpec(memory_space=pltpu...]
    ppermute x0 -> x30, waiting for transfers between devices: none -> 41.5 us  [swap(): lax.ppermute(value, axis, [(i, i ^ mask) for i in range(lax.axis_size(axi...]
    unnamed x27 -> x12, local copies, waits for them, and re-layouts: 39.8 us -> 0.03 us
    ppermute x0 -> x30, starting transfers between devices: none -> 35.9 us  [swap(): lax.ppermute(value, axis, [(i, i ^ mask) for i in range(lax.axis_size(axi...]
    slice x6 -> x3, local copies, waits for them, and re-layouts: 22.2 us -> 0.22 us  [local(): other = jnp.concatenate([other[j ^ mask(m)] for j in range(n_chip)])]
    unnamed x1 -> x0, blocking collectives: 11.8 us -> none
  transfers between devices with their start and end apart: 3 -> 30, of which waited for: 3 -> 16; matrix products, arithmetic and copies ran while one was open for 5% -> 1% of each run, Pallas kernels for 0% -> 30%
where the time goes in v2:
time: 136 us; the launch traced here: 135 us
  Pallas kernels  50.2 us (37%)
  waiting for transfers between devices  41.5 us (31%)
  starting transfers between devices  35.9 us (26%)
  other arithmetic  3.52 us (3%)
  between operations  3.52 us (3%)
    ppermute x30, waiting for transfers between devices, swap(): lax.ppermute(value, axis, [(i, i ^ mask) for i in range(lax.axis_size(axi...  41.5 us
    ppermute x30, starting transfers between devices, swap(): lax.ppermute(value, axis, [(i, i ^ mask) for i in range(lax.axis_size(axi...  35.9 us
    pallas_call x4, Pallas kernels, streamed(): pl.pallas_call(kernel, in_specs=[VMEM] + [pl.BlockSpec(memory_space=pltpu...  25.2 us
    pallas_call x2, Pallas kernels, weight_grads_chunk(): call(kernel, (depth // bm,), [pl.BlockSpec((rows, bm), lambda i: (0, i)),...  12.7 us
    pallas_call x2, Pallas kernels, down_grad_part(): call(kernel, (steps,), [pl.BlockSpec((piece.shape[0], bm), lambda i: (0,...  8.47 us
  transfers between devices with their start and end apart: 30, of which 16 were waited for; matrix products, arithmetic and copies ran while one was open for 1% of the time, Pallas kernels for 30%

profile of v2, /device:TPU:0, one launch (start us, length us, event | category | flops | bytes accessed | tf_op | source)
XLA Modules:
  0.0 135.3 jit_solution(1383076405831163823)
XLA Ops:
  0.6 3.0 %collective-permute-start = (bf16[8,2048]{1,0:T(8,128)(2,1)}, bf16[8,2048]{1,0:T(8,128)(2,1)S(1)}, u32[]{:S(2)}, u32[]{:S(2)}) collective-permute-start(bf16[8,2048]{1,0:T(8,128)(2,1)} %param.6), channel_id=1, source_target_pairs={{0,2},{1,3},{2,0},{3,1},{4,6},{5,7},{6,4},{7,5},{8,10},{9,11},{10,... | collective-permute-start | bytes 98312 | tf_op jit(solution)/shard_map/ppermute | solution.py:17
  3.9 1.8 %collective-permute-done = bf16[8,2048]{1,0:T(8,128)(2,1)S(1)} collective-permute-done((bf16[8,2048]{1,0:T(8,128)(2,1)}, bf16[8,2048]{1,0:T(8,128)(2,1)S(1)}, u32[]{:S(2)}, u32[]{:S(2)}) %collective-permute-start) | collective-permute-done | bytes 32800 | tf_op jit(solution)/shard_map/ppermute | solution.py:17
  6.5 2.0 %collective-permute-start.1 = (bf16[2,8,2048]{2,1,0:T(8,128)(2,1)S(1)}, bf16[2,8,2048]{2,1,0:T(8,128)(2,1)S(1)}, u32[]{:S(2)}, u32[]{:S(2)}) collective-permute-start(bf16[2,8,2048]{2,1,0:T(8,128)(2,1)S(1)} %pad_maximum_fusion.13), channel_id=1, source_target_pairs={{0,4},{1,5},{2,6},{3,7},{4,0},{5,1},{6,2},{7,3},{8,12},{9,13},{10,... | collective-permute-start | bytes 196616 | tf_op jit(solution)/shard_map/ppermute | solution.py:17
  8.6 4.3 %shard_map.93 = f32[64,2048]{1,0:T(8,128)S(1)} custom-call(bf16[64,2048]{1,0:T(8,128)(2,1)S(1)} %convolution_convert_fusion.x_ref, bf16[2048,2048]{1,0:T(8,128)(2,1)} %refs_0_.4), custom_call_target="tpu_custom_call" | custom-call | flops 536870912 | bytes 8388608 | tf_op jit(solution)/shard_map/pallas_call | solution.py:56
  16.5 11.1 %shard_map.94 = (f32[64,3584]{1,0:T(8,128)S(1)}, f32[64,3584]{1,0:T(8,128)S(1)}) custom-call(bf16[64,2048]{1,0:T(8,128)(2,1)S(1)} %bitcast.104, bf16[2048,3584]{1,0:T(8,128)(2,1)} %refs_0_.5, bf16[2048,3584]{1,0:T(8,128)(2,1)} %refs_1_.1), custom_call_target="tpu_custom_call" | custom-call | flops 1879048192 | bytes 29360128 | tf_op jit(solution)/shard_map/pallas_call | solution.py:56
  29.6 2.7 %collective-permute-start.6 = (bf16[2,16,3584]{2,1,0:T(8,128)(2,1)S(1)}, bf16[2,16,3584]{2,1,0:T(8,128)(2,1)S(1)}, u32[]{:S(2)}, u32[]{:S(2)}) collective-permute-start(bf16[2,16,3584]{2,1,0:T(8,128)(2,1)S(1)} %pad_maximum_fusion.5), channel_id=1, source_target_pairs={{0,16},{8,24},{16,0},{24,8},{1,17},{9,25},{17,1},{25,9},{2,18},{10... | collective-permute-start | bytes 688136 | tf_op jit(solution)/shard_map/ppermute | solution.py:17
  33.8 5.8 %collective-permute-done.5 = bf16[2,16,3584]{2,1,0:T(8,128)(2,1)S(1)} collective-permute-done((bf16[2,16,3584]{2,1,0:T(8,128)(2,1)S(1)}, bf16[2,16,3584]{2,1,0:T(8,128)(2,1)S(1)}, u32[]{:S(2)}, u32[]{:S(2)}) %collective-permute-start.5) | collective-permute-done | bytes 229408 | tf_op jit(solution)/shard_map/ppermute | solution.py:17
  39.6 9.3 %collective-permute-done.6 = bf16[2,16,3584]{2,1,0:T(8,128)(2,1)S(1)} collective-permute-done((bf16[2,16,3584]{2,1,0:T(8,128)(2,1)S(1)}, bf16[2,16,3584]{2,1,0:T(8,128)(2,1)S(1)}, u32[]{:S(2)}, u32[]{:S(2)}) %collective-permute-start.6) | collective-permute-done | bytes 229408 | tf_op jit(solution)/shard_map/ppermute | solution.py:17
  49.7 2.5 %collective-permute-start.10 = (bf16[16,3584]{1,0:T(8,128)(2,1)S(1)}, bf16[16,3584]{1,0:T(8,128)(2,1)S(1)}, u32[]{:S(2)}, u32[]{:S(2)}) collective-permute-start(bf16[16,3584]{1,0:T(8,128)(2,1)S(1)} %fusion.4.refs_0_), channel_id=1, source_target_pairs={{0,24},{8,16},{16,8},{24,0},{1,25},{9,17},{17,9},{25,1},{2,26},{10... | collective-permute-start | bytes 344072 | tf_op jit(solution)/shard_map/ppermute | solution.py:17
  52.1 4.4 %collective-permute-start.9 = (bf16[16,3584]{1,0:T(8,128)(2,1)S(1)}, bf16[16,3584]{1,0:T(8,128)(2,1)S(1)}, u32[]{:S(2)}, u32[]{:S(2)}) collective-permute-start(bf16[16,3584]{1,0:T(8,128)(2,1)S(1)} %fusion.4.refs_0_), channel_id=1, source_target_pairs={{0,16},{8,24},{16,0},{24,8},{1,17},{9,25},{17,1},{25,9},{2,18},{10... | collective-permute-start | bytes 344072 | tf_op jit(solution)/shard_map/ppermute | solution.py:17
  56.7 6.3 %collective-permute-done.9.refs_1_ = bf16[16,3584]{1,0:T(8,128)(2,1)S(1)} collective-permute-done((bf16[16,3584]{1,0:T(8,128)(2,1)S(1)}, bf16[16,3584]{1,0:T(8,128)(2,1)S(1)}, u32[]{:S(2)}, u32[]{:S(2)}) %collective-permute-start.9) | collective-permute-done | bytes 114720 | tf_op jit(solution)/shard_map/ppermute | solution.py:17
  63.0 2.6 %shard_map.96 = (f32[32,2048]{1,0:T(8,128)S(1)}, f32[32,2048]{1,0:T(8,128)S(1)}) custom-call(bf16[16,3584]{1,0:T(8,128)(2,1)S(1)} %fusion.4.refs_0_, bf16[16,3584]{1,0:T(8,128)(2,1)S(1)} %collective-permute-done.9.refs_1_, bf16[16,3584]{1,0:T(8,128)(2,1)S(1)} %collective-permute-done.8.refs_2_, bf16[16,3584]{1,0:T(8,128)(2,1)S(1)} %collective-permute-done.10.refs_3_, ...), custom_call_target="tpu_custom_call" | custom-call | flops 939524096 | bytes 14680064 | tf_op jit(solution)/shard_map/pallas_call | solution.py:163
  69.9 3.1 %collective-permute-done.13 = f32[16,2048]{1,0:T(8,128)S(1)} collective-permute-done((f32[16,2048]{1,0:T(8,128)S(1)}, f32[16,2048]{1,0:T(8,128)S(1)}, u32[]{:S(2)}, u32[]{:S(2)}) %collective-permute-start.13) | collective-permute-done | bytes 131104 | tf_op jit(solution)/shard_map/ppermute | solution.py:17
  76.3 5.9 %collective-permute-done.17 = bf16[2,16,3584]{2,1,0:T(8,128)(2,1)S(1)} collective-permute-done((bf16[2,16,3584]{2,1,0:T(8,128)(2,1)S(1)}, bf16[2,16,3584]{2,1,0:T(8,128)(2,1)S(1)}, u32[]{:S(2)}, u32[]{:S(2)}) %collective-permute-start.17) | collective-permute-done | bytes 229408 | tf_op jit(solution)/shard_map/ppermute | solution.py:17
  84.5 1.8 %collective-permute-start.19 = (f32[32,5]{0,1:T(8,128)S(1)}, f32[32,5]{0,1:T(8,128)S(1)}, u32[]{:S(2)}, u32[]{:S(2)}) collective-permute-start(f32[32,5]{0,1:T(8,128)S(1)} %concatenate.51), channel_id=1, source_target_pairs={{0,16},{8,24},{16,0},{24,8},{1,17},{9,25},{17,1},{25,9},{2,18},{10... | collective-permute-start | bytes 1928 | tf_op jit(solution)/shard_map/ppermute | solution.py:17
  86.6 1.7 %collective-permute-done.20 = f32[32,5]{0,1:T(8,128)S(1)} collective-permute-done((f32[32,5]{0,1:T(8,128)S(1)}, f32[32,5]{0,1:T(8,128)S(1)}, u32[]{:S(2)}, u32[]{:S(2)}) %collective-permute-start.20) | collective-permute-done | bytes 672 | tf_op jit(solution)/shard_map/ppermute | solution.py:17
  91.9 4.9 %shard_map.97 = (f32[32,1792]{1,0:T(8,128)S(1)}, bf16[32,1792]{1,0:T(8,128)(2,1)S(1)}) custom-call(bf16[64,2048]{1,0:T(8,128)(2,1)S(1)} %bitcast.100, bf16[3584,2048]{1,0:T(8,128)(2,1)} %refs_0_.7), custom_call_target="tpu_custom_call" | custom-call | flops 469762048 | bytes 7340032 | tf_op jit(solution)/shard_map/pallas_call | solution.py:56
  97.8 4.8 %shard_map.98 = (f32[32,1792]{1,0:T(8,128)S(1)}, bf16[32,1792]{1,0:T(8,128)(2,1)S(1)}) custom-call(bf16[64,2048]{1,0:T(8,128)(2,1)S(1)} %bitcast.101, bf16[3584,2048]{1,0:T(8,128)(2,1)} %refs_0_.7), custom_call_target="tpu_custom_call" | custom-call | flops 469762048 | bytes 7340032 | tf_op jit(solution)/shard_map/pallas_call | solution.py:56
  103.0 1.7 %collective-permute-start.24 = (bf16[32,1792]{1,0:T(8,128)(2,1)S(1)}, bf16[32,1792]{1,0:T(8,128)(2,1)S(1)}, u32[]{:S(2)}, u32[]{:S(2)}) collective-permute-start(bf16[32,1792]{1,0:T(8,128)(2,1)S(1)} %pad_maximum_fusion.11), channel_id=1, source_target_pairs={{0,16},{8,24},{16,0},{24,8},{1,17},{9,25},{17,1},{25,9},{2,18},{10... | collective-permute-start | bytes 344072 | tf_op jit(solution)/shard_map/ppermute | solution.py:17
  106.7 4.2 %shard_map.99.refs_5_ = bf16[3584,2048]{1,0:T(8,128)(2,1)} custom-call(bf16[16,3584]{1,0:T(8,128)(2,1)S(1)} %fusion.4.refs_0_, bf16[16,3584]{1,0:T(8,128)(2,1)S(1)} %collective-permute-done.9.refs_1_, bf16[16,3584]{1,0:T(8,128)(2,1)S(1)} %collective-permute-done.8.refs_2_, bf16[16,3584]{1,0:T(8,128)(2,1)S(1)} %collective-permute-done.10.refs_3_, ...), custom_call_target="tpu_custom_call" | custom-call | flops 469762048 | bytes 7340032 | tf_op jit(solution)/shard_map/pallas_call | solution.py:243
  114.4 4.2 %shard_map.100 = bf16[3584,2048]{1,0:T(8,128)(2,1)} custom-call(bf16[16,3584]{1,0:T(8,128)(2,1)S(1)} %fusion.4.refs_0_, bf16[16,3584]{1,0:T(8,128)(2,1)S(1)} %collective-permute-done.9.refs_1_, bf16[16,3584]{1,0:T(8,128)(2,1)S(1)} %collective-permute-done.8.refs_2_, ...), custom_call_target="tpu_custom_call", output_to_operand_aliasing={{}: (5, {})} | custom-call | flops 469762048 | bytes 7340032 | tf_op jit(solution)/shard_map/pallas_call | solution.py:243
  118.6 2.7 %collective-permute-done.28 = bf16[32,1792]{1,0:T(8,128)(2,1)S(1)} collective-permute-done((bf16[32,1792]{1,0:T(8,128)(2,1)S(1)}, bf16[32,1792]{1,0:T(8,128)(2,1)S(1)}, u32[]{:S(2)}, u32[]{:S(2)}) %collective-permute-start.28) | collective-permute-done | bytes 114720 | tf_op jit(solution)/shard_map/ppermute | solution.py:17
  121.4 6.4 %shard_map.101 = (bf16[2048,3584]{1,0:T(8,128)(2,1)}, bf16[2048,3584]{1,0:T(8,128)(2,1)}) custom-call(bf16[64,2048]{1,0:T(8,128)(2,1)S(1)} %bitcast.105, bf16[64,1792]{1,0:T(8,128)(2,1)S(1)} %pad_maximum_fusion.8.h_ref, bf16[2,64,3584]{2,1,0:T(8,128)(2,1)S(1)} %pad_maximum_fusion.s_ref), custom_call_target="tpu_custom_call" | custom-call | flops 939524096 | bytes 14680064 | tf_op jit(solution)/shard_map/pallas_call | solution.py:214
  127.8 6.4 %shard_map.102 = (bf16[2048,3584]{1,0:T(8,128)(2,1)}, bf16[2048,3584]{1,0:T(8,128)(2,1)}) custom-call(bf16[64,2048]{1,0:T(8,128)(2,1)S(1)} %bitcast.106, bf16[64,1792]{1,0:T(8,128)(2,1)S(1)} %pad_maximum_fusion.9.h_ref, bf16[2,64,3584]{2,1,0:T(8,128)(2,1)S(1)} %pad_maximum_fusion.s_ref, ...), custom_call_target="tpu_custom_call", output_to_operand_aliasing={{0}: (3, {}), {1}: (4, {})} | custom-call | flops 939524096 | bytes 14680064 | tf_op jit(solution)/shard_map/pallas_call | solution.py:214
  (117 shorter events, 28.1 us)
Async XLA Ops:
  0.6 5.1 %collective-permute-start = (bf16[8,2048]{1,0:T(8,128)(2,1)}, bf16[8,2048]{1,0:T(8,128)(2,1)S(1)}, u32[]{:S(2)}, u32[]{:S(2)}) collective-permute-start(bf16[8,2048]{1,0:T(8,128)(2,1)} %param.6), channel_id=1, source_target_pairs={{0,2},{1,3},{2,0},{3,1},{4,6},{5,7},{6,4},{7,5},{8,10},{9,11},{10,... | collective-permute-start | bytes 98312 | tf_op jit(solution)/shard_map/ppermute | solution.py:17
  6.5 6.4 %collective-permute-start.1 = (bf16[2,8,2048]{2,1,0:T(8,128)(2,1)S(1)}, bf16[2,8,2048]{2,1,0:T(8,128)(2,1)S(1)}, u32[]{:S(2)}, u32[]{:S(2)}) collective-permute-start(bf16[2,8,2048]{2,1,0:T(8,128)(2,1)S(1)} %pad_maximum_fusion.13), channel_id=1, source_target_pairs={{0,4},{1,5},{2,6},{3,7},{4,0},{5,1},{6,2},{7,3},{8,12},{9,13},{10,... | collective-permute-start | bytes 196616 | tf_op jit(solution)/shard_map/ppermute | solution.py:17
  15.0 12.7 %collective-permute-start.4 = (f32[32,2048]{1,0:T(8,128)S(1)}, f32[32,2048]{1,0:T(8,128)S(1)}, u32[]{:S(2)}, u32[]{:S(2)}) collective-permute-start(f32[32,2048]{1,0:T(8,128)S(1)} %fusion.2), channel_id=1, source_target_pairs={{0,2},{1,3},{2,0},{3,1},{4,6},{5,7},{6,4},{7,5},{8,10},{9,11},{10,... | collective-permute-start | bytes 786440 | tf_op jit(solution)/shard_map/ppermute | solution.py:17
  27.9 11.7 %collective-permute-start.5 = (bf16[2,16,3584]{2,1,0:T(8,128)(2,1)S(1)}, bf16[2,16,3584]{2,1,0:T(8,128)(2,1)S(1)}, u32[]{:S(2)}, u32[]{:S(2)}) collective-permute-start(bf16[2,16,3584]{2,1,0:T(8,128)(2,1)S(1)} %pad_maximum_fusion.4), channel_id=1, source_target_pairs={{0,8},{8,0},{16,24},{24,16},{1,9},{9,1},{17,25},{25,17},{2,10},{10... | collective-permute-start | bytes 688136 | tf_op jit(solution)/shard_map/ppermute | solution.py:17
  29.6 19.3 %collective-permute-start.6 = (bf16[2,16,3584]{2,1,0:T(8,128)(2,1)S(1)}, bf16[2,16,3584]{2,1,0:T(8,128)(2,1)S(1)}, u32[]{:S(2)}, u32[]{:S(2)}) collective-permute-start(bf16[2,16,3584]{2,1,0:T(8,128)(2,1)S(1)} %pad_maximum_fusion.5), channel_id=1, source_target_pairs={{0,16},{8,24},{16,0},{24,8},{1,17},{9,25},{17,1},{25,9},{2,18},{10... | collective-permute-start | bytes 688136 | tf_op jit(solution)/shard_map/ppermute | solution.py:17
  32.3 16.6 %collective-permute-start.7 = (bf16[2,16,3584]{2,1,0:T(8,128)(2,1)S(1)}, bf16[2,16,3584]{2,1,0:T(8,128)(2,1)S(1)}, u32[]{:S(2)}, u32[]{:S(2)}) collective-permute-start(bf16[2,16,3584]{2,1,0:T(8,128)(2,1)S(1)} %pad_maximum_fusion.6), channel_id=1, source_target_pairs={{0,24},{8,16},{16,8},{24,0},{1,25},{9,17},{17,9},{25,1},{2,26},{10... | collective-permute-start | bytes 688136 | tf_op jit(solution)/shard_map/ppermute | solution.py:17
  49.1 7.6 %collective-permute-start.11 = (f32[32,2048]{1,0:T(8,128)S(1)}, f32[32,2048]{1,0:T(8,128)S(1)}, u32[]{:S(2)}, u32[]{:S(2)}) collective-permute-start(f32[32,2048]{1,0:T(8,128)S(1)} %add.158), channel_id=1, source_target_pairs={{0,4},{1,5},{2,6},{3,7},{4,0},{5,1},{6,2},{7,3},{8,12},{9,13},{10,... | collective-permute-start | bytes 786440 | tf_op jit(solution)/shard_map/ppermute | solution.py:17
  49.7 7.0 %collective-permute-start.10 = (bf16[16,3584]{1,0:T(8,128)(2,1)S(1)}, bf16[16,3584]{1,0:T(8,128)(2,1)S(1)}, u32[]{:S(2)}, u32[]{:S(2)}) collective-permute-start(bf16[16,3584]{1,0:T(8,128)(2,1)S(1)} %fusion.4.refs_0_), channel_id=1, source_target_pairs={{0,24},{8,16},{16,8},{24,0},{1,25},{9,17},{17,9},{25,1},{2,26},{10... | collective-permute-start | bytes 344072 | tf_op jit(solution)/shard_map/ppermute | solution.py:17
  52.1 10.9 %collective-permute-start.9 = (bf16[16,3584]{1,0:T(8,128)(2,1)S(1)}, bf16[16,3584]{1,0:T(8,128)(2,1)S(1)}, u32[]{:S(2)}, u32[]{:S(2)}) collective-permute-start(bf16[16,3584]{1,0:T(8,128)(2,1)S(1)} %fusion.4.refs_0_), channel_id=1, source_target_pairs={{0,16},{8,24},{16,0},{24,8},{1,17},{9,25},{17,1},{25,9},{2,18},{10... | collective-permute-start | bytes 344072 | tf_op jit(solution)/shard_map/ppermute | solution.py:17
  56.5 6.5 %collective-permute-start.8 = (bf16[16,3584]{1,0:T(8,128)(2,1)S(1)}, bf16[16,3584]{1,0:T(8,128)(2,1)S(1)}, u32[]{:S(2)}, u32[]{:S(2)}) collective-permute-start(bf16[16,3584]{1,0:T(8,128)(2,1)S(1)} %fusion.4.refs_0_), channel_id=1, source_target_pairs={{0,8},{8,0},{16,24},{24,16},{1,9},{9,1},{17,25},{25,17},{2,10},{10... | collective-permute-start | bytes 344072 | tf_op jit(solution)/shard_map/ppermute | solution.py:17
  67.4 5.6 %collective-permute-start.13 = (f32[16,2048]{1,0:T(8,128)S(1)}, f32[16,2048]{1,0:T(8,128)S(1)}, u32[]{:S(2)}, u32[]{:S(2)}) collective-permute-start(f32[16,2048]{1,0:T(8,128)S(1)} %get-tuple-element.142), channel_id=1, source_target_pairs={{0,2},{1,3},{2,0},{3,1},{4,6},{5,7},{6,4},{7,5},{8,10},{9,11},{10,... | collective-permute-start | bytes 393224 | tf_op jit(solution)/shard_map/ppermute | solution.py:17
  67.5 5.5 %collective-permute-start.15 = (f32[16,2048]{1,0:T(8,128)S(1)}, f32[16,2048]{1,0:T(8,128)S(1)}, u32[]{:S(2)}, u32[]{:S(2)}) collective-permute-start(f32[16,2048]{1,0:T(8,128)S(1)} %get-tuple-element.143), channel_id=1, source_target_pairs={{0,4},{1,5},{2,6},{3,7},{4,0},{5,1},{6,2},{7,3},{8,12},{9,13},{10,... | collective-permute-start | bytes 393224 | tf_op jit(solution)/shard_map/ppermute | solution.py:17
  69.0 13.1 %collective-permute-start.17 = (bf16[2,16,3584]{2,1,0:T(8,128)(2,1)S(1)}, bf16[2,16,3584]{2,1,0:T(8,128)(2,1)S(1)}, u32[]{:S(2)}, u32[]{:S(2)}) collective-permute-start(bf16[2,16,3584]{2,1,0:T(8,128)(2,1)S(1)} %pad_maximum_fusion.7), channel_id=1, source_target_pairs={{0,16},{8,24},{16,0},{24,8},{1,17},{9,25},{17,1},{25,9},{2,18},{10... | collective-permute-start | bytes 688136 | tf_op jit(solution)/shard_map/ppermute | solution.py:17
  73.1 9.1 %collective-permute-start.14 = (f32[16,2048]{1,0:T(8,128)S(1)}, f32[16,2048]{1,0:T(8,128)S(1)}, u32[]{:S(2)}, u32[]{:S(2)}) collective-permute-start(f32[16,2048]{1,0:T(8,128)S(1)} %get-tuple-element.140), channel_id=1, source_target_pairs={{0,4},{1,5},{2,6},{3,7},{4,0},{5,1},{6,2},{7,3},{8,12},{9,13},{10,... | collective-permute-start | bytes 393224 | tf_op jit(solution)/shard_map/ppermute | solution.py:17
  74.7 7.6 %collective-permute-start.16 = (f32[16,2048]{1,0:T(8,128)S(1)}, f32[16,2048]{1,0:T(8,128)S(1)}, u32[]{:S(2)}, u32[]{:S(2)}) collective-permute-start(f32[16,2048]{1,0:T(8,128)S(1)} %get-tuple-element.141), channel_id=1, source_target_pairs={{0,2},{1,3},{2,0},{3,1},{4,6},{5,7},{6,4},{7,5},{8,10},{9,11},{10,... | collective-permute-start | bytes 393224 | tf_op jit(solution)/shard_map/ppermute | solution.py:17
  82.8 5.5 %collective-permute-start.20 = (f32[32,5]{0,1:T(8,128)S(1)}, f32[32,5]{0,1:T(8,128)S(1)}, u32[]{:S(2)}, u32[]{:S(2)}) collective-permute-start(f32[32,5]{0,1:T(8,128)S(1)} %concatenate.51), channel_id=1, source_target_pairs={{0,24},{8,16},{16,8},{24,0},{1,25},{9,17},{17,9},{25,1},{2,26},{10... | collective-permute-start | bytes 1928 | tf_op jit(solution)/shard_map/ppermute | solution.py:17
  84.5 4.5 %collective-permute-start.19 = (f32[32,5]{0,1:T(8,128)S(1)}, f32[32,5]{0,1:T(8,128)S(1)}, u32[]{:S(2)}, u32[]{:S(2)}) collective-permute-start(f32[32,5]{0,1:T(8,128)S(1)} %concatenate.51), channel_id=1, source_target_pairs={{0,16},{8,24},{16,0},{24,8},{1,17},{9,25},{17,1},{25,9},{2,18},{10... | collective-permute-start | bytes 1928 | tf_op jit(solution)/shard_map/ppermute | solution.py:17
  89.4 13.3 %collective-permute-start.23 = (bf16[2,32,3584]{2,1,0:T(8,128)(2,1)S(1)}, bf16[2,32,3584]{2,1,0:T(8,128)(2,1)S(1)}, u32[]{:S(2)}, u32[]{:S(2)}) collective-permute-start(bf16[2,32,3584]{2,1,0:T(8,128)(2,1)S(1)} %pad_maximum_fusion.1), channel_id=1, source_target_pairs={{0,8},{8,0},{16,24},{24,16},{1,9},{9,1},{17,25},{25,17},{2,10},{10... | collective-permute-start | bytes 1376264 | tf_op jit(solution)/shard_map/ppermute | solution.py:17
  96.7 6.2 %collective-permute-start.22 = (bf16[32,1792]{1,0:T(8,128)(2,1)S(1)}, bf16[32,1792]{1,0:T(8,128)(2,1)S(1)}, u32[]{:S(2)}, u32[]{:S(2)}) collective-permute-start(bf16[32,1792]{1,0:T(8,128)(2,1)S(1)} %get-tuple-element.89), channel_id=1, source_target_pairs={{0,8},{8,0},{16,24},{24,16},{1,9},{9,1},{17,25},{25,17},{2,10},{10... | collective-permute-start | bytes 344072 | tf_op jit(solution)/shard_map/ppermute | solution.py:17
  103.0 9.2 %collective-permute-start.24 = (bf16[32,1792]{1,0:T(8,128)(2,1)S(1)}, bf16[32,1792]{1,0:T(8,128)(2,1)S(1)}, u32[]{:S(2)}, u32[]{:S(2)}) collective-permute-start(bf16[32,1792]{1,0:T(8,128)(2,1)S(1)} %pad_maximum_fusion.11), channel_id=1, source_target_pairs={{0,16},{8,24},{16,0},{24,8},{1,17},{9,25},{17,1},{25,9},{2,18},{10... | collective-permute-start | bytes 344072 | tf_op jit(solution)/shard_map/ppermute | solution.py:17
  104.7 7.5 %collective-permute-start.25 = (bf16[32,1792]{1,0:T(8,128)(2,1)S(1)}, bf16[32,1792]{1,0:T(8,128)(2,1)S(1)}, u32[]{:S(2)}, u32[]{:S(2)}) collective-permute-start(bf16[32,1792]{1,0:T(8,128)(2,1)S(1)} %get-tuple-element.98), channel_id=1, source_target_pairs={{0,8},{8,0},{16,24},{24,16},{1,9},{9,1},{17,25},{25,17},{2,10},{10... | collective-permute-start | bytes 344072 | tf_op jit(solution)/shard_map/ppermute | solution.py:17
  112.3 9.0 %collective-permute-start.28 = (bf16[32,1792]{1,0:T(8,128)(2,1)S(1)}, bf16[32,1792]{1,0:T(8,128)(2,1)S(1)}, u32[]{:S(2)}, u32[]{:S(2)}) collective-permute-start(bf16[32,1792]{1,0:T(8,128)(2,1)S(1)} %pad_maximum_fusion.12), channel_id=1, source_target_pairs={{0,16},{8,24},{16,0},{24,8},{1,17},{9,25},{17,1},{25,9},{2,18},{10... | collective-permute-start | bytes 344072 | tf_op jit(solution)/shard_map/ppermute | solution.py:17
  113.2 8.1 %collective-permute-start.27 = (bf16[32,1792]{1,0:T(8,128)(2,1)S(1)}, bf16[32,1792]{1,0:T(8,128)(2,1)S(1)}, u32[]{:S(2)}, u32[]{:S(2)}) collective-permute-start(bf16[32,1792]{1,0:T(8,128)(2,1)S(1)} %add_convert_fusion.1), channel_id=1, source_target_pairs={{0,8},{8,0},{16,24},{24,16},{1,9},{9,1},{17,25},{25,17},{2,10},{10... | collective-permute-start | bytes 344072 | tf_op jit(solution)/shard_map/ppermute | solution.py:17
  121.3 6.5 %collective-permute-start.29 = (bf16[32,1792]{1,0:T(8,128)(2,1)S(1)}, bf16[32,1792]{1,0:T(8,128)(2,1)S(1)}, u32[]{:S(2)}, u32[]{:S(2)}) collective-permute-start(bf16[32,1792]{1,0:T(8,128)(2,1)S(1)} %add_convert_fusion), channel_id=1, source_target_pairs={{0,8},{8,0},{16,24},{24,16},{1,9},{9,1},{17,25},{25,17},{2,10},{10... | collective-permute-start | bytes 344072 | tf_op jit(solution)/shard_map/ppermute | solution.py:17
  (12 other events, 94.1 us)

commit v3 on v2

--- a/solution.py
+++ b/solution.py
@@ -67,21 +67,24 @@
     )(x, *[in_hbm(w) for w in weights])
 
 
-def products(x, *weights):
+def products(x, *weights, columns=None):
     depth, width = weights[0].shape
+    first, width = columns or (0, width)
     if width % 128:
-        return [jnp.dot(x, w, preferred_element_type=F32) for w in weights]
+        return [jnp.dot(x, w[:, first : first + width], preferred_element_type=F32) for w in weights]
     pieces = []
     for which in range(len(weights)):
         cuts = spans(0, width) if which == 0 else [(at, at + 896) for at in range(0, width, 896)]
-        pieces += [(which, (slice(0, depth), slice(at, min(to, width)))) for at, to in cuts]
+        pieces += [
+            (which, (slice(0, depth), slice(first + at, first + min(to, width)))) for at, to in cuts
+        ]
 
     def product(left, piece):
         return jnp.dot(left, piece, preferred_element_type=F32)
 
     def store(refs, n, part):
-        which, (_, columns) = pieces[n]
-        refs[which][:, columns] = part
+        which, (_, cut) = pieces[n]
+        refs[which][:, cut.start - first : cut.stop - first] = part
 
     shape = jax.ShapeDtypeStruct((x.shape[0], width), F32)
     return streamed(x, weights, pieces, product, [shape] * len(weights), store)
@@ -180,20 +183,24 @@
         rows_k = w_down[k * cw : (k + 1) * cw]
         part = lax.dot_general(stud_grad, rows_k, dims, preferred_element_type=F32)
         return part[:half], part[half:].astype(BF16)
-    start = k * cw
-    pieces = [(0, (slice(at, to), slice(0, width))) for at, to in spans(start, start + cw)]
-
-    def product(left, piece):
-        return lax.dot_general(left, piece, dims, preferred_element_type=F32)
-
-    def store(refs, n, part):
-        rows_n = pieces[n][1][0]
-        columns = slice(rows_n.start - start, rows_n.stop - start)
-        refs[0][:, columns] = part[:half]
-        refs[1][:, columns] = part[half:].astype(BF16)
-
-    shapes = [jax.ShapeDtypeStruct((half, cw), F32), jax.ShapeDtypeStruct((half, cw), BF16)]
-    return streamed(stud_grad, [w_down], pieces, product, shapes, store)
+    steps = steps_of(cw, 896)
+    bn = cw // steps
+
+    def kernel(g_ref, w_ref, keep_ref, send_ref):
+        part = lax.dot_general(g_ref[...], w_ref[...], dims, preferred_element_type=F32)
+        keep_ref[...] = part[:half]
+        send_ref[...] = part[half:].astype(BF16)
+
+    out = pl.BlockSpec((half, bn), lambda j: (0, j))
+    return call(
+        kernel,
+        (steps,),
+        [whole(stud_grad), pl.BlockSpec((bn, width), lambda j: (k * steps + j, 0))],
+        [out, out],
+        [jax.ShapeDtypeStruct((half, cw), F32), jax.ShapeDtypeStruct((half, cw), BF16)],
+        2 * rows * cw * width,
+        2 * cw * width,
+    )(stud_grad, w_down)
 
 
 def weight_grads_chunk(x, hidden_grad, slopes, k, cw, before):
@@ -301,11 +308,15 @@
         return [part + swap(part, "col", 1 << bit) for part, bit in zip(parts, bits)]
 
     teacher = reorder(teacher_hidden, mask(row_me), core_me)
+    teacher_parts = []
     x = student_in
     for s in reversed(range(chip_bits)):
-        x, teacher = beside(jnp.stack([x, swap(x, "col", 2 << (chip_bits - 1 - s))]), teacher)
-        if s == chip_bits - 1:
-            teacher = products(teacher, proj)[0]
+        x = jnp.stack([x, swap(x, "col", 2 << (chip_bits - 1 - s))])
+        if len(teacher_parts) < 2:
+            cut = (len(teacher_parts) * (width // 2), width // 2)
+            part = products(after(teacher, teacher_parts), proj, columns=cut)[0]
+            x, part = beside(x, part)
+            teacher_parts.append(part)
     for s in range(chip_bits):
         flag = (chip_me >> (chip_bits - 1 - s)) % 2 == 1
         if s < row_bits:
@@ -314,7 +325,7 @@
         x = jnp.where(flag, jnp.concatenate([second, first], s), x)
     x = x.reshape(n_chip, 1, own, width)
     x = jnp.concatenate([x, swap(x, "col", 1)], axis=1).reshape(tokens, width)
-    teacher = halves(teacher, n_chip)
+    teacher = halves(jnp.concatenate(teacher_parts, axis=1), n_chip)
     teacher = teacher[0] + swap(teacher[1], "col", 1)
     x, teacher = beside(x, teacher)
 
@@ -405,7 +416,7 @@
         if 0 <= t - chunks < chunks:
             k = t - chunks
             made["grad_down"] = down_grad_part(after(hidden, tie), stud_grad, k, chunks, grad_down)
-        if t == chunks:
+        if t == chunks + 1:
             made["loss"] = loss + swap(after(loss, tie), "col", 1)
         if t == chunks + transfers - 1 and chunks > 1:
             made["grads"] = weight_grads_chunk(x, after(send[0], tie), slopes, 0, cw, None)

time: 136 us -> 134 us (0.985)
  waiting for transfers between devices: 41.5 us -> 39.4 us
    pallas_call x0 -> x2, Pallas kernels: none -> 9.07 us  [hidden_grad_chunk(): call(kernel, (steps,), [whole(stud_grad), pl.BlockSpec((bn, width), lambd...]
    pallas_call x4 -> x3, Pallas kernels: 25.2 us -> 16.9 us  [streamed(): pl.pallas_call(kernel, in_specs=[VMEM] + [pl.BlockSpec(memory_space=pltpu...]
    ppermute x30, waiting for transfers between devices: 41.5 us -> 39.4 us  [swap(): lax.ppermute(value, axis, [(i, i ^ mask) for i in range(lax.axis_size(axi...]
  transfers between devices with their start and end apart: 30 -> 30, of which waited for: 16 -> 16; matrix products, arithmetic and copies ran while one was open for 1% -> 1% of each run, Pallas kernels for 30% -> 31%
where the time goes in v3:
time: 134 us; the launch traced here: 133 us
  Pallas kernels  51 us (38%)
  waiting for transfers between devices  39.4 us (29%)
  starting transfers between devices  35.3 us (26%)
  other arithmetic  3.54 us (3%)
  between operations  3.53 us (3%)
    ppermute x30, waiting for transfers between devices, swap(): lax.ppermute(value, axis, [(i, i ^ mask) for i in range(lax.axis_size(axi...  39.4 us
    ppermute x30, starting transfers between devices, swap(): lax.ppermute(value, axis, [(i, i ^ mask) for i in range(lax.axis_size(axi...  35.3 us
    pallas_call x3, Pallas kernels, streamed(): pl.pallas_call(kernel, in_specs=[VMEM] + [pl.BlockSpec(memory_space=pltpu...  16.9 us
    pallas_call x2, Pallas kernels, weight_grads_chunk(): call(kernel, (depth // bm,), [pl.BlockSpec((rows, bm), lambda i: (0, i)),...  12.7 us
    pallas_call x2, Pallas kernels, hidden_grad_chunk(): call(kernel, (steps,), [whole(stud_grad), pl.BlockSpec((bn, width), lambd...  9.07 us
    pallas_call x2, Pallas kernels, down_grad_part(): call(kernel, (steps,), [pl.BlockSpec((piece.shape[0], bm), lambda i: (0,...  8.47 us
  transfers between devices with their start and end apart: 30, of which 16 were waited for; matrix products, arithmetic and copies ran while one was open for 1% of the time, Pallas kernels for 31%

profile of v3, /device:TPU:0, one launch (start us, length us, event | category | flops | bytes accessed | tf_op | source)
XLA Modules:
  0.0 133.4 jit_solution(16647592997129737946)
XLA Ops:
  0.6 3.0 %collective-permute-start = (bf16[8,2048]{1,0:T(8,128)(2,1)}, bf16[8,2048]{1,0:T(8,128)(2,1)S(1)}, u32[]{:S(2)}, u32[]{:S(2)}) collective-permute-start(bf16[8,2048]{1,0:T(8,128)(2,1)} %param.6), channel_id=1, source_target_pairs={{0,2},{1,3},{2,0},{3,1},{4,6},{5,7},{6,4},{7,5},{8,10},{9,11},{10,... | collective-permute-start | bytes 98312 | tf_op jit(solution)/shard_map/ppermute | solution.py:17
  3.9 3.0 %shard_map.93 = f32[64,1024]{1,0:T(8,128)S(1)} custom-call(bf16[64,2048]{1,0:T(8,128)(2,1)S(1)} %convolution_convert_fusion.x_ref, bf16[2048,2048]{1,0:T(8,128)(2,1)} %refs_0_.4), custom_call_target="tpu_custom_call" | custom-call | flops 268435456 | bytes 4194304 | tf_op jit(solution)/shard_map/pallas_call | solution.py:56
  9.3 3.0 %shard_map.94 = f32[64,1024]{1,0:T(8,128)S(1)} custom-call(bf16[64,2048]{1,0:T(8,128)(2,1)S(1)} %convolution_convert_fusion.x_ref, bf16[2048,2048]{1,0:T(8,128)(2,1)} %refs_0_.4), custom_call_target="tpu_custom_call" | custom-call | flops 268435456 | bytes 4194304 | tf_op jit(solution)/shard_map/pallas_call | solution.py:56
  15.3 10.9 %shard_map.95 = (f32[64,3584]{1,0:T(8,128)S(1)}, f32[64,3584]{1,0:T(8,128)S(1)}) custom-call(bf16[64,2048]{1,0:T(8,128)(2,1)S(1)} %bitcast.104, bf16[2048,3584]{1,0:T(8,128)(2,1)} %refs_0_.5, bf16[2048,3584]{1,0:T(8,128)(2,1)} %refs_1_.1), custom_call_target="tpu_custom_call" | custom-call | flops 1879048192 | bytes 29360128 | tf_op jit(solution)/shard_map/pallas_call | solution.py:56
  26.4 1.6 %collective-permute-start.5 = (bf16[2,16,3584]{2,1,0:T(8,128)(2,1)S(1)}, bf16[2,16,3584]{2,1,0:T(8,128)(2,1)S(1)}, u32[]{:S(2)}, u32[]{:S(2)}) collective-permute-start(bf16[2,16,3584]{2,1,0:T(8,128)(2,1)S(1)} %pad_maximum_fusion.5), channel_id=1, source_target_pairs={{0,8},{8,0},{16,24},{24,16},{1,9},{9,1},{17,25},{25,17},{2,10},{10... | collective-permute-start | bytes 688136 | tf_op jit(solution)/shard_map/ppermute | solution.py:17
  28.1 2.7 %collective-permute-start.6 = (bf16[2,16,3584]{2,1,0:T(8,128)(2,1)S(1)}, bf16[2,16,3584]{2,1,0:T(8,128)(2,1)S(1)}, u32[]{:S(2)}, u32[]{:S(2)}) collective-permute-start(bf16[2,16,3584]{2,1,0:T(8,128)(2,1)S(1)} %pad_maximum_fusion.6), channel_id=1, source_target_pairs={{0,16},{8,24},{16,0},{24,8},{1,17},{9,25},{17,1},{25,9},{2,18},{10... | collective-permute-start | bytes 688136 | tf_op jit(solution)/shard_map/ppermute | solution.py:17
  32.3 5.8 %collective-permute-done.5 = bf16[2,16,3584]{2,1,0:T(8,128)(2,1)S(1)} collective-permute-done((bf16[2,16,3584]{2,1,0:T(8,128)(2,1)S(1)}, bf16[2,16,3584]{2,1,0:T(8,128)(2,1)S(1)}, u32[]{:S(2)}, u32[]{:S(2)}) %collective-permute-start.5) | collective-permute-done | bytes 229408 | tf_op jit(solution)/shard_map/ppermute | solution.py:17
  38.1 9.3 %collective-permute-done.6 = bf16[2,16,3584]{2,1,0:T(8,128)(2,1)S(1)} collective-permute-done((bf16[2,16,3584]{2,1,0:T(8,128)(2,1)S(1)}, bf16[2,16,3584]{2,1,0:T(8,128)(2,1)S(1)}, u32[]{:S(2)}, u32[]{:S(2)}) %collective-permute-start.6) | collective-permute-done | bytes 229408 | tf_op jit(solution)/shard_map/ppermute | solution.py:17
  48.9 2.5 %collective-permute-start.10 = (bf16[16,3584]{1,0:T(8,128)(2,1)S(1)}, bf16[16,3584]{1,0:T(8,128)(2,1)S(1)}, u32[]{:S(2)}, u32[]{:S(2)}) collective-permute-start(bf16[16,3584]{1,0:T(8,128)(2,1)S(1)} %fusion.4.refs_0_), channel_id=1, source_target_pairs={{0,24},{8,16},{16,8},{24,0},{1,25},{9,17},{17,9},{25,1},{2,26},{10... | collective-permute-start | bytes 344072 | tf_op jit(solution)/shard_map/ppermute | solution.py:17
  51.4 4.4 %collective-permute-start.9 = (bf16[16,3584]{1,0:T(8,128)(2,1)S(1)}, bf16[16,3584]{1,0:T(8,128)(2,1)S(1)}, u32[]{:S(2)}, u32[]{:S(2)}) collective-permute-start(bf16[16,3584]{1,0:T(8,128)(2,1)S(1)} %fusion.4.refs_0_), channel_id=1, source_target_pairs={{0,16},{8,24},{16,0},{24,8},{1,17},{9,25},{17,1},{25,9},{2,18},{10... | collective-permute-start | bytes 344072 | tf_op jit(solution)/shard_map/ppermute | solution.py:17
  55.9 6.3 %collective-permute-done.9.refs_1_ = bf16[16,3584]{1,0:T(8,128)(2,1)S(1)} collective-permute-done((bf16[16,3584]{1,0:T(8,128)(2,1)S(1)}, bf16[16,3584]{1,0:T(8,128)(2,1)S(1)}, u32[]{:S(2)}, u32[]{:S(2)}) %collective-permute-start.9) | collective-permute-done | bytes 114720 | tf_op jit(solution)/shard_map/ppermute | solution.py:17
  62.3 2.6 %shard_map.97 = (f32[32,2048]{1,0:T(8,128)S(1)}, f32[32,2048]{1,0:T(8,128)S(1)}) custom-call(bf16[16,3584]{1,0:T(8,128)(2,1)S(1)} %fusion.4.refs_0_, bf16[16,3584]{1,0:T(8,128)(2,1)S(1)} %collective-permute-done.9.refs_1_, bf16[16,3584]{1,0:T(8,128)(2,1)S(1)} %collective-permute-done.8.refs_2_, bf16[16,3584]{1,0:T(8,128)(2,1)S(1)} %collective-permute-done.10.refs_3_, ...), custom_call_target="tpu_custom_call" | custom-call | flops 939524096 | bytes 14680064 | tf_op jit(solution)/shard_map/pallas_call | solution.py:166
  69.6 2.6 %collective-permute-done.13 = f32[16,2048]{1,0:T(8,128)S(1)} collective-permute-done((f32[16,2048]{1,0:T(8,128)S(1)}, f32[16,2048]{1,0:T(8,128)S(1)}, u32[]{:S(2)}, u32[]{:S(2)}) %collective-permute-start.13) | collective-permute-done | bytes 131104 | tf_op jit(solution)/shard_map/ppermute | solution.py:17
  74.8 6.8 %collective-permute-done.17 = bf16[2,16,3584]{2,1,0:T(8,128)(2,1)S(1)} collective-permute-done((bf16[2,16,3584]{2,1,0:T(8,128)(2,1)S(1)}, bf16[2,16,3584]{2,1,0:T(8,128)(2,1)S(1)}, u32[]{:S(2)}, u32[]{:S(2)}) %collective-permute-start.17) | collective-permute-done | bytes 229408 | tf_op jit(solution)/shard_map/ppermute | solution.py:17
  82.3 1.7 %collective-permute-start.20 = (f32[32,5]{0,1:T(8,128)S(1)}, f32[32,5]{0,1:T(8,128)S(1)}, u32[]{:S(2)}, u32[]{:S(2)}) collective-permute-start(f32[32,5]{0,1:T(8,128)S(1)} %concatenate.55), channel_id=1, source_target_pairs={{0,24},{8,16},{16,8},{24,0},{1,25},{9,17},{17,9},{25,1},{2,26},{10... | collective-permute-start | bytes 1928 | tf_op jit(solution)/shard_map/ppermute | solution.py:17
  83.9 1.8 %collective-permute-start.19 = (f32[32,5]{0,1:T(8,128)S(1)}, f32[32,5]{0,1:T(8,128)S(1)}, u32[]{:S(2)}, u32[]{:S(2)}) collective-permute-start(f32[32,5]{0,1:T(8,128)S(1)} %concatenate.55), channel_id=1, source_target_pairs={{0,16},{8,24},{16,0},{24,8},{1,17},{9,25},{17,1},{25,9},{2,18},{10... | collective-permute-start | bytes 1928 | tf_op jit(solution)/shard_map/ppermute | solution.py:17
  86.0 1.7 %collective-permute-done.20 = f32[32,5]{0,1:T(8,128)S(1)} collective-permute-done((f32[32,5]{0,1:T(8,128)S(1)}, f32[32,5]{0,1:T(8,128)S(1)}, u32[]{:S(2)}, u32[]{:S(2)}) %collective-permute-start.20) | collective-permute-done | bytes 672 | tf_op jit(solution)/shard_map/ppermute | solution.py:17
  91.3 4.5 %shard_map.98 = (f32[32,1792]{1,0:T(8,128)S(1)}, bf16[32,1792]{1,0:T(8,128)(2,1)S(1)}) custom-call(bf16[64,2048]{1,0:T(8,128)(2,1)S(1)} %bitcast.100, bf16[3584,2048]{1,0:T(8,128)(2,1)} %w_ref.3), custom_call_target="tpu_custom_call" | custom-call | flops 469762048 | bytes 7340032 | tf_op jit(solution)/shard_map/pallas_call | solution.py:195
  96.9 4.5 %shard_map.99 = (f32[32,1792]{1,0:T(8,128)S(1)}, bf16[32,1792]{1,0:T(8,128)(2,1)S(1)}) custom-call(bf16[64,2048]{1,0:T(8,128)(2,1)S(1)} %bitcast.101, bf16[3584,2048]{1,0:T(8,128)(2,1)} %w_ref.3), custom_call_target="tpu_custom_call" | custom-call | flops 469762048 | bytes 7340032 | tf_op jit(solution)/shard_map/pallas_call | solution.py:195
  105.5 4.2 %shard_map.100.refs_5_ = bf16[3584,2048]{1,0:T(8,128)(2,1)} custom-call(bf16[16,3584]{1,0:T(8,128)(2,1)S(1)} %fusion.4.refs_0_, bf16[16,3584]{1,0:T(8,128)(2,1)S(1)} %collective-permute-done.9.refs_1_, bf16[16,3584]{1,0:T(8,128)(2,1)S(1)} %collective-permute-done.8.refs_2_, bf16[16,3584]{1,0:T(8,128)(2,1)S(1)} %collective-permute-done.10.refs_3_, ...), custom_call_target="tpu_custom_call" | custom-call | flops 469762048 | bytes 7340032 | tf_op jit(solution)/shard_map/pallas_call | solution.py:250
  111.2 1.7 %collective-permute-start.26 = (bf16[32,1792]{1,0:T(8,128)(2,1)S(1)}, bf16[32,1792]{1,0:T(8,128)(2,1)S(1)}, u32[]{:S(2)}, u32[]{:S(2)}) collective-permute-start(bf16[32,1792]{1,0:T(8,128)(2,1)S(1)} %add_convert_fusion.1), channel_id=1, source_target_pairs={{0,8},{8,0},{16,24},{24,16},{1,9},{9,1},{17,25},{25,17},{2,10},{10... | collective-permute-start | bytes 344072 | tf_op jit(solution)/shard_map/ppermute | solution.py:17
  113.6 4.2 %shard_map.101 = bf16[3584,2048]{1,0:T(8,128)(2,1)} custom-call(bf16[16,3584]{1,0:T(8,128)(2,1)S(1)} %fusion.4.refs_0_, bf16[16,3584]{1,0:T(8,128)(2,1)S(1)} %collective-permute-done.9.refs_1_, bf16[16,3584]{1,0:T(8,128)(2,1)S(1)} %collective-permute-done.8.refs_2_, ...), custom_call_target="tpu_custom_call", output_to_operand_aliasing={{}: (5, {})} | custom-call | flops 469762048 | bytes 7340032 | tf_op jit(solution)/shard_map/pallas_call | solution.py:250
  119.5 6.4 %shard_map.102 = (bf16[2048,3584]{1,0:T(8,128)(2,1)}, bf16[2048,3584]{1,0:T(8,128)(2,1)}) custom-call(bf16[64,2048]{1,0:T(8,128)(2,1)S(1)} %bitcast.105, bf16[64,1792]{1,0:T(8,128)(2,1)S(1)} %pad_maximum_fusion.9.h_ref, bf16[2,64,3584]{2,1,0:T(8,128)(2,1)S(1)} %pad_maximum_fusion.s_ref), custom_call_target="tpu_custom_call" | custom-call | flops 939524096 | bytes 14680064 | tf_op jit(solution)/shard_map/pallas_call | solution.py:221
  125.9 6.4 %shard_map.103 = (bf16[2048,3584]{1,0:T(8,128)(2,1)}, bf16[2048,3584]{1,0:T(8,128)(2,1)}) custom-call(bf16[64,2048]{1,0:T(8,128)(2,1)S(1)} %bitcast.106, bf16[64,1792]{1,0:T(8,128)(2,1)S(1)} %pad_maximum_fusion.10.h_ref, bf16[2,64,3584]{2,1,0:T(8,128)(2,1)S(1)} %pad_maximum_fusion.s_ref, ...), custom_call_target="tpu_custom_call", output_to_operand_aliasing={{0}: (3, {}), {1}: (4, {})} | custom-call | flops 939524096 | bytes 14680064 | tf_op jit(solution)/shard_map/pallas_call | solution.py:221
  (119 shorter events, 28.2 us)
Async XLA Ops:
  0.6 6.3 %collective-permute-start = (bf16[8,2048]{1,0:T(8,128)(2,1)}, bf16[8,2048]{1,0:T(8,128)(2,1)S(1)}, u32[]{:S(2)}, u32[]{:S(2)}) collective-permute-start(bf16[8,2048]{1,0:T(8,128)(2,1)} %param.6), channel_id=1, source_target_pairs={{0,2},{1,3},{2,0},{3,1},{4,6},{5,7},{6,4},{7,5},{8,10},{9,11},{10,... | collective-permute-start | bytes 98312 | tf_op jit(solution)/shard_map/ppermute | solution.py:17
  7.7 4.5 %collective-permute-start.1 = (bf16[2,8,2048]{2,1,0:T(8,128)(2,1)S(1)}, bf16[2,8,2048]{2,1,0:T(8,128)(2,1)S(1)}, u32[]{:S(2)}, u32[]{:S(2)}) collective-permute-start(bf16[2,8,2048]{2,1,0:T(8,128)(2,1)S(1)} %pad_maximum_fusion.14), channel_id=1, source_target_pairs={{0,4},{1,5},{2,6},{3,7},{4,0},{5,1},{6,2},{7,3},{8,12},{9,13},{10,... | collective-permute-start | bytes 196616 | tf_op jit(solution)/shard_map/ppermute | solution.py:17
  14.4 11.8 %collective-permute-start.4 = (f32[32,2048]{1,0:T(8,128)S(1)}, f32[32,2048]{1,0:T(8,128)S(1)}, u32[]{:S(2)}, u32[]{:S(2)}) collective-permute-start(f32[32,2048]{1,0:T(8,128)S(1)} %fusion.2), channel_id=1, source_target_pairs={{0,2},{1,3},{2,0},{3,1},{4,6},{5,7},{6,4},{7,5},{8,10},{9,11},{10,... | collective-permute-start | bytes 786440 | tf_op jit(solution)/shard_map/ppermute | solution.py:17
  26.4 11.7 %collective-permute-start.5 = (bf16[2,16,3584]{2,1,0:T(8,128)(2,1)S(1)}, bf16[2,16,3584]{2,1,0:T(8,128)(2,1)S(1)}, u32[]{:S(2)}, u32[]{:S(2)}) collective-permute-start(bf16[2,16,3584]{2,1,0:T(8,128)(2,1)S(1)} %pad_maximum_fusion.5), channel_id=1, source_target_pairs={{0,8},{8,0},{16,24},{24,16},{1,9},{9,1},{17,25},{25,17},{2,10},{10... | collective-permute-start | bytes 688136 | tf_op jit(solution)/shard_map/ppermute | solution.py:17
  28.1 19.3 %collective-permute-start.6 = (bf16[2,16,3584]{2,1,0:T(8,128)(2,1)S(1)}, bf16[2,16,3584]{2,1,0:T(8,128)(2,1)S(1)}, u32[]{:S(2)}, u32[]{:S(2)}) collective-permute-start(bf16[2,16,3584]{2,1,0:T(8,128)(2,1)S(1)} %pad_maximum_fusion.6), channel_id=1, source_target_pairs={{0,16},{8,24},{16,0},{24,8},{1,17},{9,25},{17,1},{25,9},{2,18},{10... | collective-permute-start | bytes 688136 | tf_op jit(solution)/shard_map/ppermute | solution.py:17
  30.8 16.6 %collective-permute-start.7 = (bf16[2,16,3584]{2,1,0:T(8,128)(2,1)S(1)}, bf16[2,16,3584]{2,1,0:T(8,128)(2,1)S(1)}, u32[]{:S(2)}, u32[]{:S(2)}) collective-permute-start(bf16[2,16,3584]{2,1,0:T(8,128)(2,1)S(1)} %pad_maximum_fusion.7), channel_id=1, source_target_pairs={{0,24},{8,16},{16,8},{24,0},{1,25},{9,17},{17,9},{25,1},{2,26},{10... | collective-permute-start | bytes 688136 | tf_op jit(solution)/shard_map/ppermute | solution.py:17
  47.6 8.3 %collective-permute-start.11 = (f32[32,2048]{1,0:T(8,128)S(1)}, f32[32,2048]{1,0:T(8,128)S(1)}, u32[]{:S(2)}, u32[]{:S(2)}) collective-permute-start(f32[32,2048]{1,0:T(8,128)S(1)} %add.158), channel_id=1, source_target_pairs={{0,4},{1,5},{2,6},{3,7},{4,0},{5,1},{6,2},{7,3},{8,12},{9,13},{10,... | collective-permute-start | bytes 786440 | tf_op jit(solution)/shard_map/ppermute | solution.py:17
  48.9 7.0 %collective-permute-start.10 = (bf16[16,3584]{1,0:T(8,128)(2,1)S(1)}, bf16[16,3584]{1,0:T(8,128)(2,1)S(1)}, u32[]{:S(2)}, u32[]{:S(2)}) collective-permute-start(bf16[16,3584]{1,0:T(8,128)(2,1)S(1)} %fusion.4.refs_0_), channel_id=1, source_target_pairs={{0,24},{8,16},{16,8},{24,0},{1,25},{9,17},{17,9},{25,1},{2,26},{10... | collective-permute-start | bytes 344072 | tf_op jit(solution)/shard_map/ppermute | solution.py:17
  51.4 10.9 %collective-permute-start.9 = (bf16[16,3584]{1,0:T(8,128)(2,1)S(1)}, bf16[16,3584]{1,0:T(8,128)(2,1)S(1)}, u32[]{:S(2)}, u32[]{:S(2)}) collective-permute-start(bf16[16,3584]{1,0:T(8,128)(2,1)S(1)} %fusion.4.refs_0_), channel_id=1, source_target_pairs={{0,16},{8,24},{16,0},{24,8},{1,17},{9,25},{17,1},{25,9},{2,18},{10... | collective-permute-start | bytes 344072 | tf_op jit(solution)/shard_map/ppermute | solution.py:17
  55.8 6.5 %collective-permute-start.8 = (bf16[16,3584]{1,0:T(8,128)(2,1)S(1)}, bf16[16,3584]{1,0:T(8,128)(2,1)S(1)}, u32[]{:S(2)}, u32[]{:S(2)}) collective-permute-start(bf16[16,3584]{1,0:T(8,128)(2,1)S(1)} %fusion.4.refs_0_), channel_id=1, source_target_pairs={{0,8},{8,0},{16,24},{24,16},{1,9},{9,1},{17,25},{25,17},{2,10},{10... | collective-permute-start | bytes 344072 | tf_op jit(solution)/shard_map/ppermute | solution.py:17
  66.6 5.6 %collective-permute-start.13 = (f32[16,2048]{1,0:T(8,128)S(1)}, f32[16,2048]{1,0:T(8,128)S(1)}, u32[]{:S(2)}, u32[]{:S(2)}) collective-permute-start(f32[16,2048]{1,0:T(8,128)S(1)} %get-tuple-element.144), channel_id=1, source_target_pairs={{0,2},{1,3},{2,0},{3,1},{4,6},{5,7},{6,4},{7,5},{8,10},{9,11},{10,... | collective-permute-start | bytes 393224 | tf_op jit(solution)/shard_map/ppermute | solution.py:17
  67.9 5.3 %collective-permute-start.15 = (f32[16,2048]{1,0:T(8,128)S(1)}, f32[16,2048]{1,0:T(8,128)S(1)}, u32[]{:S(2)}, u32[]{:S(2)}) collective-permute-start(f32[16,2048]{1,0:T(8,128)S(1)} %get-tuple-element.145), channel_id=1, source_target_pairs={{0,4},{1,5},{2,6},{3,7},{4,0},{5,1},{6,2},{7,3},{8,12},{9,13},{10,... | collective-permute-start | bytes 393224 | tf_op jit(solution)/shard_map/ppermute | solution.py:17
  68.8 12.8 %collective-permute-start.17 = (bf16[2,16,3584]{2,1,0:T(8,128)(2,1)S(1)}, bf16[2,16,3584]{2,1,0:T(8,128)(2,1)S(1)}, u32[]{:S(2)}, u32[]{:S(2)}) collective-permute-start(bf16[2,16,3584]{2,1,0:T(8,128)(2,1)S(1)} %pad_maximum_fusion.8), channel_id=1, source_target_pairs={{0,16},{8,24},{16,0},{24,8},{1,17},{9,25},{17,1},{25,9},{2,18},{10... | collective-permute-start | bytes 688136 | tf_op jit(solution)/shard_map/ppermute | solution.py:17
  73.2 8.4 %collective-permute-start.14 = (f32[16,2048]{1,0:T(8,128)S(1)}, f32[16,2048]{1,0:T(8,128)S(1)}, u32[]{:S(2)}, u32[]{:S(2)}) collective-permute-start(f32[16,2048]{1,0:T(8,128)S(1)} %get-tuple-element.142), channel_id=1, source_target_pairs={{0,4},{1,5},{2,6},{3,7},{4,0},{5,1},{6,2},{7,3},{8,12},{9,13},{10,... | collective-permute-start | bytes 393224 | tf_op jit(solution)/shard_map/ppermute | solution.py:17
  74.1 7.6 %collective-permute-start.16 = (f32[16,2048]{1,0:T(8,128)S(1)}, f32[16,2048]{1,0:T(8,128)S(1)}, u32[]{:S(2)}, u32[]{:S(2)}) collective-permute-start(f32[16,2048]{1,0:T(8,128)S(1)} %get-tuple-element.143), channel_id=1, source_target_pairs={{0,2},{1,3},{2,0},{3,1},{4,6},{5,7},{6,4},{7,5},{8,10},{9,11},{10,... | collective-permute-start | bytes 393224 | tf_op jit(solution)/shard_map/ppermute | solution.py:17
  82.3 5.5 %collective-permute-start.20 = (f32[32,5]{0,1:T(8,128)S(1)}, f32[32,5]{0,1:T(8,128)S(1)}, u32[]{:S(2)}, u32[]{:S(2)}) collective-permute-start(f32[32,5]{0,1:T(8,128)S(1)} %concatenate.55), channel_id=1, source_target_pairs={{0,24},{8,16},{16,8},{24,0},{1,25},{9,17},{17,9},{25,1},{2,26},{10... | collective-permute-start | bytes 1928 | tf_op jit(solution)/shard_map/ppermute | solution.py:17
  83.9 4.5 %collective-permute-start.19 = (f32[32,5]{0,1:T(8,128)S(1)}, f32[32,5]{0,1:T(8,128)S(1)}, u32[]{:S(2)}, u32[]{:S(2)}) collective-permute-start(f32[32,5]{0,1:T(8,128)S(1)} %concatenate.55), channel_id=1, source_target_pairs={{0,16},{8,24},{16,0},{24,8},{1,17},{9,25},{17,1},{25,9},{2,18},{10... | collective-permute-start | bytes 1928 | tf_op jit(solution)/shard_map/ppermute | solution.py:17
  88.8 12.6 %collective-permute-start.23 = (bf16[2,32,3584]{2,1,0:T(8,128)(2,1)S(1)}, bf16[2,32,3584]{2,1,0:T(8,128)(2,1)S(1)}, u32[]{:S(2)}, u32[]{:S(2)}) collective-permute-start(bf16[2,32,3584]{2,1,0:T(8,128)(2,1)S(1)} %pad_maximum_fusion.2), channel_id=1, source_target_pairs={{0,8},{8,0},{16,24},{24,16},{1,9},{9,1},{17,25},{25,17},{2,10},{10... | collective-permute-start | bytes 1376264 | tf_op jit(solution)/shard_map/ppermute | solution.py:17
  95.9 6.5 %collective-permute-start.22 = (bf16[32,1792]{1,0:T(8,128)(2,1)S(1)}, bf16[32,1792]{1,0:T(8,128)(2,1)S(1)}, u32[]{:S(2)}, u32[]{:S(2)}) collective-permute-start(bf16[32,1792]{1,0:T(8,128)(2,1)S(1)} %get-tuple-element.91), channel_id=1, source_target_pairs={{0,8},{8,0},{16,24},{24,16},{1,9},{9,1},{17,25},{25,17},{2,10},{10... | collective-permute-start | bytes 344072 | tf_op jit(solution)/shard_map/ppermute | solution.py:17
  102.4 7.6 %collective-permute-start.24 = (bf16[32,1792]{1,0:T(8,128)(2,1)S(1)}, bf16[32,1792]{1,0:T(8,128)(2,1)S(1)}, u32[]{:S(2)}, u32[]{:S(2)}) collective-permute-start(bf16[32,1792]{1,0:T(8,128)(2,1)S(1)} %pad_maximum_fusion.12), channel_id=1, source_target_pairs={{0,16},{8,24},{16,0},{24,8},{1,17},{9,25},{17,1},{25,9},{2,18},{10... | collective-permute-start | bytes 344072 | tf_op jit(solution)/shard_map/ppermute | solution.py:17
  104.0 6.1 %collective-permute-start.25 = (bf16[32,1792]{1,0:T(8,128)(2,1)S(1)}, bf16[32,1792]{1,0:T(8,128)(2,1)S(1)}, u32[]{:S(2)}, u32[]{:S(2)}) collective-permute-start(bf16[32,1792]{1,0:T(8,128)(2,1)S(1)} %get-tuple-element.100), channel_id=1, source_target_pairs={{0,8},{8,0},{16,24},{24,16},{1,9},{9,1},{17,25},{25,17},{2,10},{10... | collective-permute-start | bytes 344072 | tf_op jit(solution)/shard_map/ppermute | solution.py:17
  110.2 8.8 %collective-permute-start.27 = (bf16[32,1792]{1,0:T(8,128)(2,1)S(1)}, bf16[32,1792]{1,0:T(8,128)(2,1)S(1)}, u32[]{:S(2)}, u32[]{:S(2)}) collective-permute-start(bf16[32,1792]{1,0:T(8,128)(2,1)S(1)} %pad_maximum_fusion.13), channel_id=1, source_target_pairs={{0,16},{8,24},{16,0},{24,8},{1,17},{9,25},{17,1},{25,9},{2,18},{10... | collective-permute-start | bytes 344072 | tf_op jit(solution)/shard_map/ppermute | solution.py:17
  111.2 7.9 %collective-permute-start.26 = (bf16[32,1792]{1,0:T(8,128)(2,1)S(1)}, bf16[32,1792]{1,0:T(8,128)(2,1)S(1)}, u32[]{:S(2)}, u32[]{:S(2)}) collective-permute-start(bf16[32,1792]{1,0:T(8,128)(2,1)S(1)} %add_convert_fusion.1), channel_id=1, source_target_pairs={{0,8},{8,0},{16,24},{24,16},{1,9},{9,1},{17,25},{25,17},{2,10},{10... | collective-permute-start | bytes 344072 | tf_op jit(solution)/shard_map/ppermute | solution.py:17
  119.1 6.8 %collective-permute-start.29 = (bf16[32,1792]{1,0:T(8,128)(2,1)S(1)}, bf16[32,1792]{1,0:T(8,128)(2,1)S(1)}, u32[]{:S(2)}, u32[]{:S(2)}) collective-permute-start(bf16[32,1792]{1,0:T(8,128)(2,1)S(1)} %add_convert_fusion), channel_id=1, source_target_pairs={{0,8},{8,0},{16,24},{24,16},{1,9},{9,1},{17,25},{25,17},{2,10},{10... | collective-permute-start | bytes 344072 | tf_op jit(solution)/shard_map/ppermute | solution.py:17
  (12 other events, 90.6 us)

commit v4 on v3

--- a/solution.py
+++ b/solution.py
@@ -331,16 +331,20 @@
 
     q = tokens // n_row
     teacher = teacher + swap(teacher, "col", 2)
-    both = products(x, w_gate, w_up)
-    both, teacher = beside(both, teacher)
-    pieces = []
-    for m in range(n_row):
-        at = turned(m) * q
-        pieces.append(jnp.stack([part[at : at + q] for part in both]))
-    send = [piece.astype(BF16) for piece in pieces]
+
+    def row_pieces(part):
+        return [part[turned(m) * q : (turned(m) + 1) * q] for m in range(n_row)]
+
+    gate = row_pieces(products(x, w_gate)[0])
+    send = [piece.astype(BF16) for piece in gate]
+    up = products(after(x, send), w_up)[0]
+    arrived, (up, teacher) = beside(to_rows(send), (up, teacher))
+    gate = row_sum(gate[0], arrived)
+    up = row_pieces(up)
+    send = [piece.astype(BF16) for piece in up]
     near = fetched(w_down, send[1:]) if width_ff % 128 == 0 else w_down
     arrived, near = beside(to_rows(send), near)
-    gate, up = row_sum(pieces[0], arrived)
+    up = row_sum(up[0], arrived)
     logistic = jax.nn.sigmoid(gate)
     silu = gate * logistic
     slope = logistic * (1.0 + gate * (1.0 - logistic))

time: 134 us -> 131 us (0.978)
  waiting for transfers between devices: 39.4 us -> 34.2 us
  Pallas kernels: 51 us -> 53.2 us
    ppermute x30 -> x33, waiting for transfers between devices: 39.4 us -> 34.2 us  [swap(): lax.ppermute(value, axis, [(i, i ^ mask) for i in range(lax.axis_size(axi...]
    pallas_call x3 -> x4, Pallas kernels: 16.9 us -> 19.1 us  [streamed(): pl.pallas_call(kernel, in_specs=[VMEM] + [pl.BlockSpec(memory_space=pltpu...]
    ppermute x30 -> x33, starting transfers between devices: 35.3 us -> 36.2 us  [swap(): lax.ppermute(value, axis, [(i, i ^ mask) for i in range(lax.axis_size(axi...]
  transfers between devices with their start and end apart: 30 -> 33, of which waited for: 16 -> 18; matrix products, arithmetic and copies ran while one was open for 1% -> 1% of each run, Pallas kernels for 31% -> 34%
where the time goes in v4:
time: 131 us
  Pallas kernels  53.2 us (41%)
  starting transfers between devices  36.2 us (28%)
  waiting for transfers between devices  34.2 us (26%)
  other arithmetic  3.48 us (3%)
  between operations  3.44 us (3%)
    ppermute x33, starting transfers between devices, swap(): lax.ppermute(value, axis, [(i, i ^ mask) for i in range(lax.axis_size(axi...  36.2 us
    ppermute x33, waiting for transfers between devices, swap(): lax.ppermute(value, axis, [(i, i ^ mask) for i in range(lax.axis_size(axi...  34.2 us
    pallas_call x4, Pallas kernels, streamed(): pl.pallas_call(kernel, in_specs=[VMEM] + [pl.BlockSpec(memory_space=pltpu...  19.1 us
    pallas_call x2, Pallas kernels, weight_grads_chunk(): call(kernel, (depth // bm,), [pl.BlockSpec((rows, bm), lambda i: (0, i)),...  12.7 us
    pallas_call x2, Pallas kernels, hidden_grad_chunk(): call(kernel, (steps,), [whole(stud_grad), pl.BlockSpec((bn, width), lambd...  9.07 us
    pallas_call x2, Pallas kernels, down_grad_part(): call(kernel, (steps,), [pl.BlockSpec((piece.shape[0], bm), lambda i: (0,...  8.47 us
    pallas_call x1, Pallas kernels, down_product(): call(kernel, (), [VMEM] * (n + 1), [VMEM] * 2, [shape] * 2, 2 * rows * de...  2.63 us
  transfers between devices with their start and end apart: 33, of which 18 were waited for; matrix products, arithmetic and copies ran while one was open for 1% of the time, Pallas kernels for 34%

profile of v4, /device:TPU:0, one launch (start us, length us, event | category | flops | bytes accessed | tf_op | source)
XLA Modules:
  0.0 131.2 jit_solution(9757161897759450037)
XLA Ops:
  0.6 3.0 %collective-permute-start = (bf16[8,2048]{1,0:T(8,128)(2,1)}, bf16[8,2048]{1,0:T(8,128)(2,1)S(1)}, u32[]{:S(2)}, u32[]{:S(2)}) collective-permute-start(bf16[8,2048]{1,0:T(8,128)(2,1)} %param.6), channel_id=1, source_target_pairs={{0,2},{1,3},{2,0},{3,1},{4,6},{5,7},{6,4},{7,5},{8,10},{9,11},{10,... | collective-permute-start | bytes 98312 | tf_op jit(solution)/shard_map/ppermute | solution.py:17
  3.9 3.0 %shard_map.93 = f32[64,1024]{1,0:T(8,128)S(1)} custom-call(bf16[64,2048]{1,0:T(8,128)(2,1)S(1)} %convolution_convert_fusion.x_ref, bf16[2048,2048]{1,0:T(8,128)(2,1)} %refs_0_.5), custom_call_target="tpu_custom_call" | custom-call | flops 268435456 | bytes 4194304 | tf_op jit(solution)/shard_map/pallas_call | solution.py:56
  9.3 3.0 %shard_map.94 = f32[64,1024]{1,0:T(8,128)S(1)} custom-call(bf16[64,2048]{1,0:T(8,128)(2,1)S(1)} %convolution_convert_fusion.x_ref, bf16[2048,2048]{1,0:T(8,128)(2,1)} %refs_0_.5), custom_call_target="tpu_custom_call" | custom-call | flops 268435456 | bytes 4194304 | tf_op jit(solution)/shard_map/pallas_call | solution.py:56
  15.3 6.6 %shard_map.95 = f32[64,3584]{1,0:T(8,128)S(1)} custom-call(bf16[64,2048]{1,0:T(8,128)(2,1)S(1)} %bitcast.75, bf16[2048,3584]{1,0:T(8,128)(2,1)} %refs_0_.6), custom_call_target="tpu_custom_call" | custom-call | flops 939524096 | bytes 14680064 | tf_op jit(solution)/shard_map/pallas_call | solution.py:56
  22.0 3.7 %collective-permute-start.6 = (bf16[16,3584]{1,0:T(8,128)(2,1)S(1)}, bf16[16,3584]{1,0:T(8,128)(2,1)S(1)}, u32[]{:S(2)}, u32[]{:S(2)}) collective-permute-start(bf16[16,3584]{1,0:T(8,128)(2,1)S(1)} %get-tuple-element.141), channel_id=1, source_target_pairs={{0,24},{8,16},{16,8},{24,0},{1,25},{9,17},{17,9},{25,1},{2,26},{10... | collective-permute-start | bytes 344072 | tf_op jit(solution)/shard_map/ppermute | solution.py:17
  26.4 6.5 %shard_map.96 = f32[64,3584]{1,0:T(8,128)S(1)} custom-call(bf16[64,2048]{1,0:T(8,128)(2,1)S(1)} %bitcast.76, bf16[2048,3584]{1,0:T(8,128)(2,1)} %refs_0_.7), custom_call_target="tpu_custom_call" | custom-call | flops 939524096 | bytes 14680064 | tf_op jit(solution)/shard_map/pallas_call | solution.py:56
  33.0 2.4 %collective-permute-done.5 = bf16[16,3584]{1,0:T(8,128)(2,1)S(1)} collective-permute-done((bf16[16,3584]{1,0:T(8,128)(2,1)S(1)}, bf16[16,3584]{1,0:T(8,128)(2,1)S(1)}, u32[]{:S(2)}, u32[]{:S(2)}) %collective-permute-start.5) | collective-permute-done | bytes 114720 | tf_op jit(solution)/shard_map/ppermute | solution.py:17
  35.5 2.5 %collective-permute-start.10 = (bf16[16,3584]{1,0:T(8,128)(2,1)S(1)}, bf16[16,3584]{1,0:T(8,128)(2,1)S(1)}, u32[]{:S(2)}, u32[]{:S(2)}) collective-permute-start(bf16[16,3584]{1,0:T(8,128)(2,1)S(1)} %get-tuple-element.138), channel_id=1, source_target_pairs={{0,24},{8,16},{16,8},{24,0},{1,25},{9,17},{17,9},{25,1},{2,26},{10... | collective-permute-start | bytes 344072 | tf_op jit(solution)/shard_map/ppermute | solution.py:17
  38.1 1.9 %collective-permute-start.8 = (bf16[16,3584]{1,0:T(8,128)(2,1)S(1)}, bf16[16,3584]{1,0:T(8,128)(2,1)S(1)}, u32[]{:S(2)}, u32[]{:S(2)}) collective-permute-start(bf16[16,3584]{1,0:T(8,128)(2,1)S(1)} %get-tuple-element.140), channel_id=1, source_target_pairs={{0,8},{8,0},{16,24},{24,16},{1,9},{9,1},{17,25},{25,17},{2,10},{10... | collective-permute-start | bytes 344072 | tf_op jit(solution)/shard_map/ppermute | solution.py:17
  41.2 2.3 %collective-permute-done.10 = bf16[16,3584]{1,0:T(8,128)(2,1)S(1)} collective-permute-done((bf16[16,3584]{1,0:T(8,128)(2,1)S(1)}, bf16[16,3584]{1,0:T(8,128)(2,1)S(1)}, u32[]{:S(2)}, u32[]{:S(2)}) %collective-permute-start.10) | collective-permute-done | bytes 114720 | tf_op jit(solution)/shard_map/ppermute | solution.py:17
  43.5 3.9 %collective-permute-done.9 = bf16[16,3584]{1,0:T(8,128)(2,1)S(1)} collective-permute-done((bf16[16,3584]{1,0:T(8,128)(2,1)S(1)}, bf16[16,3584]{1,0:T(8,128)(2,1)S(1)}, u32[]{:S(2)}, u32[]{:S(2)}) %collective-permute-start.9) | collective-permute-done | bytes 114720 | tf_op jit(solution)/shard_map/ppermute | solution.py:17
  50.6 2.8 %collective-permute-start.11 = (bf16[16,3584]{1,0:T(8,128)(2,1)S(1)}, bf16[16,3584]{1,0:T(8,128)(2,1)S(1)}, u32[]{:S(2)}, u32[]{:S(2)}) collective-permute-start(bf16[16,3584]{1,0:T(8,128)(2,1)S(1)} %get-tuple-element.109.refs_0_), channel_id=1, source_target_pairs={{0,8},{8,0},{16,24},{24,16},{1,9},{9,1},{17,25},{25,17},{2,10},{10... | collective-permute-start | bytes 344072 | tf_op jit(solution)/shard_map/ppermute | solution.py:17
  53.3 2.0 %collective-permute-done.14 = f32[32,2048]{1,0:T(8,128)S(1)} collective-permute-done((f32[32,2048]{1,0:T(8,128)S(1)}, f32[32,2048]{1,0:T(8,128)S(1)}, u32[]{:S(2)}, u32[]{:S(2)}) %collective-permute-start.14) | collective-permute-done | bytes 262176 | tf_op jit(solution)/shard_map/ppermute | solution.py:17
  56.8 3.5 %collective-permute-done.12.refs_1_ = bf16[16,3584]{1,0:T(8,128)(2,1)S(1)} collective-permute-done((bf16[16,3584]{1,0:T(8,128)(2,1)S(1)}, bf16[16,3584]{1,0:T(8,128)(2,1)S(1)}, u32[]{:S(2)}, u32[]{:S(2)}) %collective-permute-start.12) | collective-permute-done | bytes 114720 | tf_op jit(solution)/shard_map/ppermute | solution.py:17
  60.4 2.6 %shard_map.98 = (f32[32,2048]{1,0:T(8,128)S(1)}, f32[32,2048]{1,0:T(8,128)S(1)}) custom-call(bf16[16,3584]{1,0:T(8,128)(2,1)S(1)} %get-tuple-element.109.refs_0_, bf16[16,3584]{1,0:T(8,128)(2,1)S(1)} %collective-permute-done.12.refs_1_, bf16[16,3584]{1,0:T(8,128)(2,1)S(1)} %collective-permute-done.11.refs_2_, ...), custom_call_target="tpu_custom_call" | custom-call | flops 939524096 | bytes 14680064 | tf_op jit(solution)/shard_map/pallas_call | solution.py:166
  67.2 3.1 %collective-permute-done.16 = f32[16,2048]{1,0:T(8,128)S(1)} collective-permute-done((f32[16,2048]{1,0:T(8,128)S(1)}, f32[16,2048]{1,0:T(8,128)S(1)}, u32[]{:S(2)}, u32[]{:S(2)}) %collective-permute-start.16) | collective-permute-done | bytes 131104 | tf_op jit(solution)/shard_map/ppermute | solution.py:17
  72.9 6.3 %collective-permute-done.20 = bf16[2,16,3584]{2,1,0:T(8,128)(2,1)S(1)} collective-permute-done((bf16[2,16,3584]{2,1,0:T(8,128)(2,1)S(1)}, bf16[2,16,3584]{2,1,0:T(8,128)(2,1)S(1)}, u32[]{:S(2)}, u32[]{:S(2)}) %collective-permute-start.20) | collective-permute-done | bytes 229408 | tf_op jit(solution)/shard_map/ppermute | solution.py:17
  79.9 1.9 %collective-permute-start.23 = (f32[32,5]{0,1:T(8,128)S(1)}, f32[32,5]{0,1:T(8,128)S(1)}, u32[]{:S(2)}, u32[]{:S(2)}) collective-permute-start(f32[32,5]{0,1:T(8,128)S(1)} %concatenate.55), channel_id=1, source_target_pairs={{0,24},{8,16},{16,8},{24,0},{1,25},{9,17},{17,9},{25,1},{2,26},{10... | collective-permute-start | bytes 1928 | tf_op jit(solution)/shard_map/ppermute | solution.py:17
  89.1 4.5 %shard_map.99 = (f32[32,1792]{1,0:T(8,128)S(1)}, bf16[32,1792]{1,0:T(8,128)(2,1)S(1)}) custom-call(bf16[64,2048]{1,0:T(8,128)(2,1)S(1)} %bitcast.71, bf16[3584,2048]{1,0:T(8,128)(2,1)} %w_ref.3), custom_call_target="tpu_custom_call" | custom-call | flops 469762048 | bytes 7340032 | tf_op jit(solution)/shard_map/pallas_call | solution.py:195
  94.7 4.5 %shard_map.100 = (f32[32,1792]{1,0:T(8,128)S(1)}, bf16[32,1792]{1,0:T(8,128)(2,1)S(1)}) custom-call(bf16[64,2048]{1,0:T(8,128)(2,1)S(1)} %bitcast.72, bf16[3584,2048]{1,0:T(8,128)(2,1)} %w_ref.3), custom_call_target="tpu_custom_call" | custom-call | flops 469762048 | bytes 7340032 | tf_op jit(solution)/shard_map/pallas_call | solution.py:195
  103.1 4.2 %shard_map.101.refs_5_ = bf16[3584,2048]{1,0:T(8,128)(2,1)} custom-call(bf16[16,3584]{1,0:T(8,128)(2,1)S(1)} %get-tuple-element.109.refs_0_, bf16[16,3584]{1,0:T(8,128)(2,1)S(1)} %collective-permute-done.12.refs_1_, bf16[16,3584]{1,0:T(8,128)(2,1)S(1)} %collective-permute-done.11.refs_2_, bf16[16,3584]{1,0:T(8,128)(2,1)S(1)} %collective-permute-done.13.refs_3_, ...), custom_call_target="tpu_custom_call" | custom-call | flops 469762048 | bytes 7340032 | tf_op jit(solution)/shard_map/pallas_call | solution.py:250
  111.2 4.2 %shard_map.102 = bf16[3584,2048]{1,0:T(8,128)(2,1)} custom-call(bf16[16,3584]{1,0:T(8,128)(2,1)S(1)} %get-tuple-element.109.refs_0_, bf16[16,3584]{1,0:T(8,128)(2,1)S(1)} %collective-permute-done.12.refs_1_, bf16[16,3584]{1,0:T(8,128)(2,1)S(1)} %collective-permute-done.11.refs_2_, ...), custom_call_target="tpu_custom_call", output_to_operand_aliasing={{}: (5, {})} | custom-call | flops 469762048 | bytes 7340032 | tf_op jit(solution)/shard_map/pallas_call | solution.py:250
  117.3 6.4 %shard_map.103 = (bf16[2048,3584]{1,0:T(8,128)(2,1)}, bf16[2048,3584]{1,0:T(8,128)(2,1)}) custom-call(bf16[64,2048]{1,0:T(8,128)(2,1)S(1)} %bitcast.77, bf16[64,1792]{1,0:T(8,128)(2,1)S(1)} %pad_maximum_fusion.6.h_ref, bf16[2,64,3584]{2,1,0:T(8,128)(2,1)S(1)} %pad_maximum_fusion.s_ref), custom_call_target="tpu_custom_call" | custom-call | flops 939524096 | bytes 14680064 | tf_op jit(solution)/shard_map/pallas_call | solution.py:221
  123.7 6.4 %shard_map.104 = (bf16[2048,3584]{1,0:T(8,128)(2,1)}, bf16[2048,3584]{1,0:T(8,128)(2,1)}) custom-call(bf16[64,2048]{1,0:T(8,128)(2,1)S(1)} %bitcast.78, bf16[64,1792]{1,0:T(8,128)(2,1)S(1)} %pad_maximum_fusion.7.h_ref, bf16[2,64,3584]{2,1,0:T(8,128)(2,1)S(1)} %pad_maximum_fusion.s_ref, ...), custom_call_target="tpu_custom_call", output_to_operand_aliasing={{0}: (3, {}), {1}: (4, {})} | custom-call | flops 939524096 | bytes 14680064 | tf_op jit(solution)/shard_map/pallas_call | solution.py:221
  (121 shorter events, 36.4 us)
Async XLA Ops:
  0.6 6.3 %collective-permute-start = (bf16[8,2048]{1,0:T(8,128)(2,1)}, bf16[8,2048]{1,0:T(8,128)(2,1)S(1)}, u32[]{:S(2)}, u32[]{:S(2)}) collective-permute-start(bf16[8,2048]{1,0:T(8,128)(2,1)} %param.6), channel_id=1, source_target_pairs={{0,2},{1,3},{2,0},{3,1},{4,6},{5,7},{6,4},{7,5},{8,10},{9,11},{10,... | collective-permute-start | bytes 98312 | tf_op jit(solution)/shard_map/ppermute | solution.py:17
  14.3 18.6 %collective-permute-start.7 = (f32[32,2048]{1,0:T(8,128)S(1)}, f32[32,2048]{1,0:T(8,128)S(1)}, u32[]{:S(2)}, u32[]{:S(2)}) collective-permute-start(f32[32,2048]{1,0:T(8,128)S(1)} %fusion), channel_id=1, source_target_pairs={{0,2},{1,3},{2,0},{3,1},{4,6},{5,7},{6,4},{7,5},{8,10},{9,11},{10,... | collective-permute-start | bytes 786440 | tf_op jit(solution)/shard_map/ppermute | solution.py:17
  22.0 11.0 %collective-permute-start.6 = (bf16[16,3584]{1,0:T(8,128)(2,1)S(1)}, bf16[16,3584]{1,0:T(8,128)(2,1)S(1)}, u32[]{:S(2)}, u32[]{:S(2)}) collective-permute-start(bf16[16,3584]{1,0:T(8,128)(2,1)S(1)} %get-tuple-element.141), channel_id=1, source_target_pairs={{0,24},{8,16},{16,8},{24,0},{1,25},{9,17},{17,9},{25,1},{2,26},{10... | collective-permute-start | bytes 344072 | tf_op jit(solution)/shard_map/ppermute | solution.py:17
  25.7 9.8 %collective-permute-start.5 = (bf16[16,3584]{1,0:T(8,128)(2,1)S(1)}, bf16[16,3584]{1,0:T(8,128)(2,1)S(1)}, u32[]{:S(2)}, u32[]{:S(2)}) collective-permute-start(bf16[16,3584]{1,0:T(8,128)(2,1)S(1)} %get-tuple-element.142), channel_id=1, source_target_pairs={{0,16},{8,24},{16,0},{24,8},{1,17},{9,25},{17,1},{25,9},{2,18},{10... | collective-permute-start | bytes 344072 | tf_op jit(solution)/shard_map/ppermute | solution.py:17
  25.7 9.8 %collective-permute-start.4 = (bf16[16,3584]{1,0:T(8,128)(2,1)S(1)}, bf16[16,3584]{1,0:T(8,128)(2,1)S(1)}, u32[]{:S(2)}, u32[]{:S(2)}) collective-permute-start(bf16[16,3584]{1,0:T(8,128)(2,1)S(1)} %get-tuple-element.143), channel_id=1, source_target_pairs={{0,8},{8,0},{16,24},{24,16},{1,9},{9,1},{17,25},{25,17},{2,10},{10... | collective-permute-start | bytes 344072 | tf_op jit(solution)/shard_map/ppermute | solution.py:17
  35.5 7.9 %collective-permute-start.10 = (bf16[16,3584]{1,0:T(8,128)(2,1)S(1)}, bf16[16,3584]{1,0:T(8,128)(2,1)S(1)}, u32[]{:S(2)}, u32[]{:S(2)}) collective-permute-start(bf16[16,3584]{1,0:T(8,128)(2,1)S(1)} %get-tuple-element.138), channel_id=1, source_target_pairs={{0,24},{8,16},{16,8},{24,0},{1,25},{9,17},{17,9},{25,1},{2,26},{10... | collective-permute-start | bytes 344072 | tf_op jit(solution)/shard_map/ppermute | solution.py:17
  38.1 9.3 %collective-permute-start.9 = (bf16[16,3584]{1,0:T(8,128)(2,1)S(1)}, bf16[16,3584]{1,0:T(8,128)(2,1)S(1)}, u32[]{:S(2)}, u32[]{:S(2)}) collective-permute-start(bf16[16,3584]{1,0:T(8,128)(2,1)S(1)} %get-tuple-element.139), channel_id=1, source_target_pairs={{0,16},{8,24},{16,0},{24,8},{1,17},{9,25},{17,1},{25,9},{2,18},{10... | collective-permute-start | bytes 344072 | tf_op jit(solution)/shard_map/ppermute | solution.py:17
  38.1 9.3 %collective-permute-start.8 = (bf16[16,3584]{1,0:T(8,128)(2,1)S(1)}, bf16[16,3584]{1,0:T(8,128)(2,1)S(1)}, u32[]{:S(2)}, u32[]{:S(2)}) collective-permute-start(bf16[16,3584]{1,0:T(8,128)(2,1)S(1)} %get-tuple-element.140), channel_id=1, source_target_pairs={{0,8},{8,0},{16,24},{24,16},{1,9},{9,1},{17,25},{25,17},{2,10},{10... | collective-permute-start | bytes 344072 | tf_op jit(solution)/shard_map/ppermute | solution.py:17
  47.7 7.7 %collective-permute-start.14 = (f32[32,2048]{1,0:T(8,128)S(1)}, f32[32,2048]{1,0:T(8,128)S(1)}, u32[]{:S(2)}, u32[]{:S(2)}) collective-permute-start(f32[32,2048]{1,0:T(8,128)S(1)} %add.162), channel_id=1, source_target_pairs={{0,4},{1,5},{2,6},{3,7},{4,0},{5,1},{6,2},{7,3},{8,12},{9,13},{10,... | collective-permute-start | bytes 786440 | tf_op jit(solution)/shard_map/ppermute | solution.py:17
  49.0 7.9 %collective-permute-start.13 = (bf16[16,3584]{1,0:T(8,128)(2,1)S(1)}, bf16[16,3584]{1,0:T(8,128)(2,1)S(1)}, u32[]{:S(2)}, u32[]{:S(2)}) collective-permute-start(bf16[16,3584]{1,0:T(8,128)(2,1)S(1)} %get-tuple-element.109.refs_0_), channel_id=1, source_target_pairs={{0,24},{8,16},{16,8},{24,0},{1,25},{9,17},{17,9},{25,1},{2,26},{10... | collective-permute-start | bytes 344072 | tf_op jit(solution)/shard_map/ppermute | solution.py:17
  50.6 9.8 %collective-permute-start.12 = (bf16[16,3584]{1,0:T(8,128)(2,1)S(1)}, bf16[16,3584]{1,0:T(8,128)(2,1)S(1)}, u32[]{:S(2)}, u32[]{:S(2)}) collective-permute-start(bf16[16,3584]{1,0:T(8,128)(2,1)S(1)} %get-tuple-element.109.refs_0_), channel_id=1, source_target_pairs={{0,16},{8,24},{16,0},{24,8},{1,17},{9,25},{17,1},{25,9},{2,18},{10... | collective-permute-start | bytes 344072 | tf_op jit(solution)/shard_map/ppermute | solution.py:17
  50.6 9.8 %collective-permute-start.11 = (bf16[16,3584]{1,0:T(8,128)(2,1)S(1)}, bf16[16,3584]{1,0:T(8,128)(2,1)S(1)}, u32[]{:S(2)}, u32[]{:S(2)}) collective-permute-start(bf16[16,3584]{1,0:T(8,128)(2,1)S(1)} %get-tuple-element.109.refs_0_), channel_id=1, source_target_pairs={{0,8},{8,0},{16,24},{24,16},{1,9},{9,1},{17,25},{25,17},{2,10},{10... | collective-permute-start | bytes 344072 | tf_op jit(solution)/shard_map/ppermute | solution.py:17
  64.7 5.6 %collective-permute-start.16 = (f32[16,2048]{1,0:T(8,128)S(1)}, f32[16,2048]{1,0:T(8,128)S(1)}, u32[]{:S(2)}, u32[]{:S(2)}) collective-permute-start(f32[16,2048]{1,0:T(8,128)S(1)} %get-tuple-element.146), channel_id=1, source_target_pairs={{0,2},{1,3},{2,0},{3,1},{4,6},{5,7},{6,4},{7,5},{8,10},{9,11},{10,... | collective-permute-start | bytes 393224 | tf_op jit(solution)/shard_map/ppermute | solution.py:17
  66.9 12.3 %collective-permute-start.20 = (bf16[2,16,3584]{2,1,0:T(8,128)(2,1)S(1)}, bf16[2,16,3584]{2,1,0:T(8,128)(2,1)S(1)}, u32[]{:S(2)}, u32[]{:S(2)}) collective-permute-start(bf16[2,16,3584]{2,1,0:T(8,128)(2,1)S(1)} %pad_maximum_fusion.5), channel_id=1, source_target_pairs={{0,16},{8,24},{16,0},{24,8},{1,17},{9,25},{17,1},{25,9},{2,18},{10... | collective-permute-start | bytes 688136 | tf_op jit(solution)/shard_map/ppermute | solution.py:17
  71.3 7.9 %collective-permute-start.17 = (f32[16,2048]{1,0:T(8,128)S(1)}, f32[16,2048]{1,0:T(8,128)S(1)}, u32[]{:S(2)}, u32[]{:S(2)}) collective-permute-start(f32[16,2048]{1,0:T(8,128)S(1)} %get-tuple-element.144), channel_id=1, source_target_pairs={{0,4},{1,5},{2,6},{3,7},{4,0},{5,1},{6,2},{7,3},{8,12},{9,13},{10,... | collective-permute-start | bytes 393224 | tf_op jit(solution)/shard_map/ppermute | solution.py:17
  72.2 7.1 %collective-permute-start.19 = (f32[16,2048]{1,0:T(8,128)S(1)}, f32[16,2048]{1,0:T(8,128)S(1)}, u32[]{:S(2)}, u32[]{:S(2)}) collective-permute-start(f32[16,2048]{1,0:T(8,128)S(1)} %get-tuple-element.145), channel_id=1, source_target_pairs={{0,2},{1,3},{2,0},{3,1},{4,6},{5,7},{6,4},{7,5},{8,10},{9,11},{10,... | collective-permute-start | bytes 393224 | tf_op jit(solution)/shard_map/ppermute | solution.py:17
  79.9 5.5 %collective-permute-start.23 = (f32[32,5]{0,1:T(8,128)S(1)}, f32[32,5]{0,1:T(8,128)S(1)}, u32[]{:S(2)}, u32[]{:S(2)}) collective-permute-start(f32[32,5]{0,1:T(8,128)S(1)} %concatenate.55), channel_id=1, source_target_pairs={{0,24},{8,16},{16,8},{24,0},{1,25},{9,17},{17,9},{25,1},{2,26},{10... | collective-permute-start | bytes 1928 | tf_op jit(solution)/shard_map/ppermute | solution.py:17
  86.6 12.6 %collective-permute-start.26 = (bf16[2,32,3584]{2,1,0:T(8,128)(2,1)S(1)}, bf16[2,32,3584]{2,1,0:T(8,128)(2,1)S(1)}, u32[]{:S(2)}, u32[]{:S(2)}) collective-permute-start(bf16[2,32,3584]{2,1,0:T(8,128)(2,1)S(1)} %pad_maximum_fusion.2), channel_id=1, source_target_pairs={{0,8},{8,0},{16,24},{24,16},{1,9},{9,1},{17,25},{25,17},{2,10},{10... | collective-permute-start | bytes 1376264 | tf_op jit(solution)/shard_map/ppermute | solution.py:17
  93.6 6.8 %collective-permute-start.25 = (bf16[32,1792]{1,0:T(8,128)(2,1)S(1)}, bf16[32,1792]{1,0:T(8,128)(2,1)S(1)}, u32[]{:S(2)}, u32[]{:S(2)}) collective-permute-start(bf16[32,1792]{1,0:T(8,128)(2,1)S(1)} %get-tuple-element.93), channel_id=1, source_target_pairs={{0,8},{8,0},{16,24},{24,16},{1,9},{9,1},{17,25},{25,17},{2,10},{10... | collective-permute-start | bytes 344072 | tf_op jit(solution)/shard_map/ppermute | solution.py:17
  100.5 7.3 %collective-permute-start.27 = (bf16[32,1792]{1,0:T(8,128)(2,1)S(1)}, bf16[32,1792]{1,0:T(8,128)(2,1)S(1)}, u32[]{:S(2)}, u32[]{:S(2)}) collective-permute-start(bf16[32,1792]{1,0:T(8,128)(2,1)S(1)} %pad_maximum_fusion.9), channel_id=1, source_target_pairs={{0,16},{8,24},{16,0},{24,8},{1,17},{9,25},{17,1},{25,9},{2,18},{10... | collective-permute-start | bytes 344072 | tf_op jit(solution)/shard_map/ppermute | solution.py:17
  101.6 6.2 %collective-permute-start.28 = (bf16[32,1792]{1,0:T(8,128)(2,1)S(1)}, bf16[32,1792]{1,0:T(8,128)(2,1)S(1)}, u32[]{:S(2)}, u32[]{:S(2)}) collective-permute-start(bf16[32,1792]{1,0:T(8,128)(2,1)S(1)} %get-tuple-element.102), channel_id=1, source_target_pairs={{0,8},{8,0},{16,24},{24,16},{1,9},{9,1},{17,25},{25,17},{2,10},{10... | collective-permute-start | bytes 344072 | tf_op jit(solution)/shard_map/ppermute | solution.py:17
  107.9 8.7 %collective-permute-start.30 = (bf16[32,1792]{1,0:T(8,128)(2,1)S(1)}, bf16[32,1792]{1,0:T(8,128)(2,1)S(1)}, u32[]{:S(2)}, u32[]{:S(2)}) collective-permute-start(bf16[32,1792]{1,0:T(8,128)(2,1)S(1)} %pad_maximum_fusion.10), channel_id=1, source_target_pairs={{0,16},{8,24},{16,0},{24,8},{1,17},{9,25},{17,1},{25,9},{2,18},{10... | collective-permute-start | bytes 344072 | tf_op jit(solution)/shard_map/ppermute | solution.py:17
  109.0 7.6 %collective-permute-start.29 = (bf16[32,1792]{1,0:T(8,128)(2,1)S(1)}, bf16[32,1792]{1,0:T(8,128)(2,1)S(1)}, u32[]{:S(2)}, u32[]{:S(2)}) collective-permute-start(bf16[32,1792]{1,0:T(8,128)(2,1)S(1)} %add_convert_fusion.1), channel_id=1, source_target_pairs={{0,8},{8,0},{16,24},{24,16},{1,9},{9,1},{17,25},{25,17},{2,10},{10... | collective-permute-start | bytes 344072 | tf_op jit(solution)/shard_map/ppermute | solution.py:17
  116.7 7.0 %collective-permute-start.32 = (bf16[32,1792]{1,0:T(8,128)(2,1)S(1)}, bf16[32,1792]{1,0:T(8,128)(2,1)S(1)}, u32[]{:S(2)}, u32[]{:S(2)}) collective-permute-start(bf16[32,1792]{1,0:T(8,128)(2,1)S(1)} %add_convert_fusion), channel_id=1, source_target_pairs={{0,8},{8,0},{16,24},{24,16},{1,9},{9,1},{17,25},{25,17},{2,10},{10... | collective-permute-start | bytes 344072 | tf_op jit(solution)/shard_map/ppermute | solution.py:17
  (15 other events, 117.7 us)
